TPU v7x, 32 devices: a whole 2x2x4 slice. The times are simulated.
32 devices in a mesh: band: 8 (over y, x, core), ga: 4 (over z).
Axes of the slice: x: 2, y: 2, z: 4, core: 2. Of those that a mesh axis runs over, the one named last changes fastest.
Arguments:
- coeffs: float32 [1024, 16384], P('band', 'ga'), may hold values from -90 to 90, as said below
Outputs:
- orthonormal: float32 [1024, 16384], P('band', 'ga')
Inputs may be any that keep to these rules, and one draw needn't show every extreme that they name: `coeffs`: bands are linearly independent.
All inputs are finite; a program needn't handle non-finite values.
Results may differ from a plain program's by a relative error of at most 0.00029.
Values sent between devices are 32-bit elements; how exact they have to be, the bound alone decides.
No kernel may reach another device: no remote copies, remote signals or barrier semaphores. Data moves between devices by JAX's collectives and lax.ppermute only.
A program may use at most 128 MiB of HBM per device.

v0:
```python
import functools

import jax
import jax.numpy as jnp
from jax import lax
from jax.experimental import pallas as pl
from jax.experimental.pallas import tpu as pltpu
from jax.sharding import PartitionSpec as P

BLOCK = 128
STRIP = 8
NN = (((1,), (0,)), ((), ()))
NT = (((1,), (1,)), ((), ()))


def halves(x):
    high = x.astype(jnp.bfloat16)
    return high, (x - high.astype(jnp.float32)).astype(jnp.bfloat16)


def left3(x):
    high, low = halves(x)
    return jnp.concatenate([high, low, high], axis=1)


def right3(x):
    high, low = halves(x)
    return jnp.concatenate([high, high, low], axis=0)


def right3t(x):
    high, low = halves(x)
    return jnp.concatenate([high, high, low], axis=1)


def mm(a, b, dims=NN):
    return lax.dot_general(a, b, dims, preferred_element_type=jnp.float32)


NEAR = 2


def leaf(strips, row_ref, col_ref):
    strips = list(strips)
    count = len(strips)
    shape = strips[0].shape
    lane = lax.broadcasted_iota(jnp.int32, shape, 1)
    sub = lax.broadcasted_iota(jnp.int32, shape, 0)
    each = range(STRIP)

    def column(x, c):
        return jnp.broadcast_to(x[:, c : c + 1], shape)

    def repeated(ref, r):
        return jnp.broadcast_to(ref[r : r + 1, :], shape)

    for s in range(count):
        base = STRIP * s
        row_ref[base : base + STRIP, :] = strips[s]
        for b in each:
            at = (base + b) * STRIP
            col_ref[at : at + STRIP, :] = column(strips[s], base + b)
        rows = [repeated(row_ref, base + q) for q in each]
        piv = [
            [repeated(col_ref, (base + b) * STRIP + a) if b >= a else None for b in each] for a in each
        ]
        panel = (lane >= base) & (lane < base + STRIP)
        rows = [jnp.where(panel, jnp.where(lane == base + q, 1.0, 0.0), rows[q]) for q in each]
        mult = [[None] * STRIP for _ in each]
        done = [None] * STRIP
        gain = [None] * STRIP
        for q in each:
            root = lax.rsqrt(piv[q][q])
            inv = root * root
            for a in range(q + 1, STRIP):
                mult[a][q] = piv[q][a] * inv
            for a in range(q + 1, STRIP):
                for b in range(a, STRIP):
                    piv[a][b] = piv[a][b] - mult[a][q] * piv[q][b]
                rows[a] = rows[a] - mult[a][q] * rows[q]
            gain[q] = rows[q] * inv
            done[q] = rows[q] * root
        for q in range(STRIP - 1, 0, -1):
            for a in range(q):
                gain[a] = gain[a] - mult[q][a] * gain[q]
        far = s + 1 + NEAR
        for t in range(s + 1, min(far, count)):
            terms = [column(strips[t], base + q) * gain[q] for q in each]
            while len(terms) > 1:
                terms = [terms[i] + terms[i + 1] for i in range(0, len(terms), 2)]
            strips[t] = jnp.where(panel, 0.0, strips[t]) - terms[0]
        if far < count:
            g = gain[0]
            for q in range(1, STRIP):
                g = jnp.where(sub == q, gain[q], g)
            below = STRIP * (count - s - 1)

            def padded(x):
                parts = [x]
                if base:
                    parts = [jnp.zeros((base, BLOCK), x.dtype)] + parts
                if below:
                    parts = parts + [jnp.zeros((below, BLOCK), x.dtype)]
                return jnp.concatenate(parts, axis=0)

            g_high, g_low = [padded(x) for x in halves(g)]
            s_high, s_low = halves(jnp.concatenate(strips[far:], axis=0))
            t = mm(
                jnp.concatenate([s_high, s_low], axis=1), jnp.concatenate([g_high, g_high], axis=0)
            ) + mm(s_high, g_low)
            for i in range(far, count):
                at = STRIP * (i - far)
                strips[i] = jnp.where(panel, 0.0, strips[i]) - t[at : at + STRIP, :]
        new = done[0]
        for q in range(1, STRIP):
            new = jnp.where(sub == q, done[q], new)
        strips[s] = new
    return [jnp.where(lane <= sub + STRIP * s, strips[s], 0.0) for s in range(count)]


def vmem_call(kernel, shapes, scratch, idx, operands, cost=1):
    space = pl.BlockSpec(memory_space=pltpu.VMEM)
    return pl.pallas_call(
        kernel,
        out_shape=shapes,
        in_specs=[pl.BlockSpec(memory_space=pltpu.SMEM)] + [space] * len(operands),
        out_specs=[space] * len(shapes),
        scratch_shapes=scratch,
        compiler_params=pltpu.CompilerParams(vmem_limit_bytes=40 * 2**20),
        cost_estimate=pl.CostEstimate(
            flops=cost * 1_000_000_000, bytes_accessed=0, transcendentals=0
        ),
    )(idx, *operands)


def f32(*shape):
    return jax.ShapeDtypeStruct(shape, jnp.float32)


def cut_kernel(parts, width, idx_ref, x_ref, *outs):
    for d in range(parts):
        start = pl.multiple_of(jnp.bitwise_xor(idx_ref[0], d) * width, width)
        outs[d][...] = x_ref[:, pl.ds(start, width)]


def cut_columns(x, idx, parts):
    width = x.shape[1] // parts
    return vmem_call(
        functools.partial(cut_kernel, parts, width), [f32(x.shape[0], width)] * parts, [], idx, [x]
    )


def join_kernel(parts, width, idx_ref, *refs):
    for d in range(parts):
        start = pl.multiple_of(jnp.bitwise_xor(idx_ref[0], d) * width, width)
        refs[parts][:, pl.ds(start, width)] = refs[d][...]


def join_columns(pieces, idx):
    parts = len(pieces)
    rows, width = pieces[0].shape
    return vmem_call(
        functools.partial(join_kernel, parts, width), [f32(rows, width * parts)], [], idx, pieces
    )[0]


def sum_split_kernel(terms, parts, slot, idx_ref, *refs):
    ins, outs = refs[:terms], refs[terms:]
    rows = outs[0].shape[0]
    for d in range(parts):
        part = pl.ds(pl.multiple_of(jnp.bitwise_xor(idx_ref[slot], d) * rows, 8), rows)
        total = ins[0][part, :]
        for r in ins[1:]:
            total = total + r[part, :]
        outs[d][...] = total


def sum_split(terms, parts, slot, idx):
    rows, width = terms[0].shape
    return vmem_call(
        functools.partial(sum_split_kernel, len(terms), parts, slot),
        [f32(rows // parts, width)] * parts,
        [],
        idx,
        terms,
    )


def lower_blocks(first, last):
    return [(i, j) for i in range(first, last) for j in range(i + 1)]


def gram_kernel(parts, scale, head, order, idx_ref, *refs):
    pieces = refs[:parts]
    outs = refs[parts : parts + 4]
    a_ref, b_ref, flat_ref, flat2_ref = refs[parts + 4 :]
    rows, width = pieces[0].shape
    for d in range(parts):
        at = pl.ds(pl.multiple_of(jnp.bitwise_xor(idx_ref[0], d) * rows, rows), rows)
        high, low = halves(pieces[d][...])
        a_ref[at, 0:width] = high
        a_ref[at, width : 2 * width] = low
        a_ref[at, 2 * width :] = high
        b_ref[at, 0:width] = high
        b_ref[at, width : 2 * width] = high
        b_ref[at, 2 * width :] = low
    place = {}
    for ref, blocks in ((flat_ref, lower_blocks(0, head)), (flat2_ref, lower_blocks(head, order // BLOCK))):
        for n, block in enumerate(blocks):
            half = len(blocks) // 2
            place[block] = (ref, n // half, (n % half) * BLOCK)
    wide = 2 * BLOCK
    for c in range(0, order, wide):
        t = mm(a_ref[c:, :], b_ref[c : c + wide, :], NT) * scale
        for i in range(c // BLOCK, order // BLOCK):
            for j in (c // BLOCK, c // BLOCK + 1):
                if j <= i:
                    ref, half, row = place[i, j]
                    ref[half, row : row + BLOCK, :] = t[
                        i * BLOCK - c : (i + 1) * BLOCK - c, j * BLOCK - c : (j + 1) * BLOCK - c
                    ]
    core = jnp.bitwise_and(idx_ref[0], 1)
    for ref, keep, send in ((flat_ref, outs[0], outs[1]), (flat2_ref, outs[2], outs[3])):
        keep[...] = ref[core]
        send[...] = ref[1 - core]


def gram(pieces, idx, columns_all, head):
    parts = len(pieces)
    rows, width = pieces[0].shape
    order = rows * parts
    r1 = len(lower_blocks(0, head)) * BLOCK // 2
    r2 = len(lower_blocks(head, order // BLOCK)) * BLOCK // 2
    return vmem_call(
        functools.partial(gram_kernel, parts, 1.0 / columns_all, head, order),
        [f32(r1, BLOCK), f32(r1, BLOCK), f32(r2, BLOCK), f32(r2, BLOCK)],
        [
            pltpu.VMEM((order, 3 * width), jnp.bfloat16),
            pltpu.VMEM((order, 3 * width), jnp.bfloat16),
            pltpu.VMEM((2, r1, BLOCK), jnp.float32),
            pltpu.VMEM((2, r2, BLOCK), jnp.float32),
        ],
        idx,
        pieces,
    )


def swap(x, axis, d):
    return lax.ppermute(x, axis, [(i, i ^ d) for i in range(lax.axis_size(axis))])


def after(x, y):
    return lax.optimization_barrier((x, y))[0]


def sum_all(terms):
    return sum(terms[1:], terms[0])


def sum_first(keep, send, idx):
    chips, depth = lax.axis_size("band") // 2, lax.axis_size("ga")
    pieces = sum_split([keep, swap(send, "band", 1)], chips, 1, idx)
    part = sum_all([pieces[0]] + [swap(pieces[d], "band", 2 * d) for d in range(1, chips)])
    if depth <= 4:
        total = sum_all([part] + [swap(part, "ga", d) for d in range(1, depth)])
    else:
        total = lax.psum(part, "ga")
    return lax.all_gather(total, "band", axis=0, tiled=True), (pieces[0], part, total)


def sum_second(keep, send, marks, idx):
    chips, depth = lax.axis_size("band") // 2, lax.axis_size("ga")
    pieces = sum_split([keep, swap(after(send, marks[0]), "band", 1)], chips, 1, idx)
    pieces = [pieces[0]] + [after(pieces[d], marks[1]) for d in range(1, chips)]
    plane = [pieces[0]] + [swap(pieces[d], "band", 2 * d) for d in range(1, chips)]
    if depth > 4:
        return lax.psum(sum_all(plane), "ga")
    pieces = sum_split(plane, depth, 2, idx)
    pieces = [pieces[0]] + [after(pieces[d], marks[2]) for d in range(1, depth)]
    return sum_all([pieces[0]] + [swap(pieces[d], "ga", d) for d in range(1, depth)])


def gather_ga(own, mark):
    depth = lax.axis_size("ga")
    if depth > 4:
        return own
    own = after(own, mark)
    return jnp.concatenate([own] + [swap(own, "ga", d) for d in range(1, depth)], axis=0)


def gather_chips(own, mark):
    parts = lax.axis_size("band")
    own = after(own, mark)
    groups = [list(range(core, parts, 2)) for core in range(2)]
    copies = jnp.broadcast_to(own, (parts // 2, *own.shape))
    got = lax.all_to_all(copies, "band", 0, 0, axis_index_groups=groups)
    return got.reshape(-1, own.shape[1])


def place_bands(first_ref, parts, flat_ref):
    rows = first_ref.shape[0] // parts
    for band in range(parts):
        at = ((band % 2) * (parts // 2) + band // 2) * rows
        flat_ref[at : at + rows, :] = first_ref[band * rows : (band + 1) * rows, :]


def place_offsets(halves_, chips, cuts, idx_ref, flat_ref):
    rows = halves_[0].shape[0] // (chips * cuts)
    for c, ref in enumerate(halves_):
        core = jnp.bitwise_xor(jnp.bitwise_and(idx_ref[0], 1), c)
        for chip in range(chips):
            for z in range(cuts):
                at = (core * chips + chip) * cuts
                at = at + (jnp.bitwise_xor(idx_ref[2], z) if cuts > 1 else 0)
                start = (chip * cuts + z) * rows
                flat_ref[pl.ds(pl.multiple_of(at * rows, 8), rows), :] = ref[start : start + rows, :]


def eliminate(x_ref, vl_ref, vr_ref, r_ref, row_ref, col_ref, base, lo, order):
    hi = lo + BLOCK
    wide = 2 * BLOCK
    row = slice(lo - base, hi - base)
    w = jnp.concatenate(
        leaf(
            [x_ref[lo - base + s : lo - base + s + STRIP, lo:hi] for s in range(0, BLOCK, STRIP)],
            row_ref,
            col_ref,
        ),
        axis=0,
    )
    w_left = left3(w)
    r_ref[:, lo:hi] = right3(w)
    rest = order - hi
    if rest:
        v = mm(left3(x_ref[hi - base :, lo:hi]), right3t(w), NT)
        vl_ref[:rest, :] = left3(v)
        vr_ref[:rest, :] = right3t(v)
        for c in range(hi, order, wide):
            d = min(c + wide, order)
            t = mm(vl_ref[c - hi : rest, :], vr_ref[c - hi : d - hi, :], NT)
            x_ref[c - base :, c:d] = x_ref[c - base :, c:d] - t
    for c in range(0, lo, wide):
        d = min(c + wide, lo)
        t = mm(w_left, right3(x_ref[row, c:d]))
        x_ref[row, c:d] = t
        r_ref[:, c:d] = right3(t)
    x_ref[row, lo:hi] = w
    if rest:
        x_ref[row, hi:] = jnp.zeros((BLOCK, rest), jnp.float32)
        for c in range(0, hi, wide):
            d = min(c + wide, hi)
            t = mm(vl_ref[:rest, :], r_ref[:, c:d])
            if d <= lo:
                x_ref[hi - base :, c:d] = x_ref[hi - base :, c:d] - t
            else:
                if c < lo:
                    x_ref[hi - base :, c:lo] = x_ref[hi - base :, c:lo] - t[:, : lo - c]
                x_ref[hi - base :, lo:hi] = -t[:, lo - c :]


def head_kernel(parts, head, idx_ref, first_ref, x_ref, flat_ref, *work):
    place_bands(first_ref, parts, flat_ref)
    for n, (i, j) in enumerate(lower_blocks(0, head)):
        x_ref[i * BLOCK : (i + 1) * BLOCK, j * BLOCK : (j + 1) * BLOCK] = flat_ref[
            n * BLOCK : (n + 1) * BLOCK, :
        ]
    order = head * BLOCK
    for lo in range(0, order // 2, BLOCK):
        eliminate(x_ref, *work, 0, lo, order)


def neck_kernel(head, idx_ref, in_ref, x_ref, *work):
    x_ref[...] = in_ref[...]
    order = head * BLOCK
    for lo in range(order // 2, order, BLOCK):
        eliminate(x_ref, *work, 0, lo, order)


def tail_kernel(chips, cuts, head, order, idx_ref, top_ref, near_ref, far_ref, x_ref, flat_ref, *work):
    base = head * BLOCK
    place_offsets([near_ref, far_ref], chips, cuts, idx_ref, flat_ref)
    for n, (i, j) in enumerate(lower_blocks(head, order // BLOCK)):
        x_ref[i * BLOCK - base : (i + 1) * BLOCK - base, j * BLOCK : (j + 1) * BLOCK] = flat_ref[
            n * BLOCK : (n + 1) * BLOCK, :
        ]
    top_high, top_low = halves(top_ref[...])
    s_high, s_low = halves(x_ref[:, :base])
    v = mm(s_high, top_high, NT) + mm(s_high, top_low, NT) + mm(s_low, top_high, NT)
    v_high, v_low = halves(v)
    x_ref[:, :base] = -(mm(v_high, top_high) + mm(v_high, top_low) + mm(v_low, top_high))
    x_ref[:, base:] = x_ref[:, base:] - (
        mm(v_high, v_high, NT) + mm(v_high, v_low, NT) + mm(v_low, v_high, NT)
    )
    for lo in range(base, order, BLOCK):
        eliminate(x_ref, *work, base, lo, order)


def factor_scratch(blocks, rows, order):
    return [
        pltpu.VMEM((len(blocks) * BLOCK, BLOCK), jnp.float32),
        pltpu.VMEM((rows - BLOCK, 3 * BLOCK), jnp.bfloat16),
        pltpu.VMEM((rows - BLOCK, 3 * BLOCK), jnp.bfloat16),
        pltpu.VMEM((3 * BLOCK, order), jnp.bfloat16),
        pltpu.VMEM((BLOCK, BLOCK), jnp.float32),
        pltpu.VMEM((BLOCK * STRIP, BLOCK), jnp.float32),
    ]


def head_factor(first, parts, idx, head):
    rows = head * BLOCK
    return vmem_call(
        functools.partial(head_kernel, parts, head),
        [f32(rows, rows)],
        factor_scratch(lower_blocks(0, head), rows, rows),
        idx,
        [first],
        cost=60,
    )[0]


def neck_factor(started, idx, head):
    rows = head * BLOCK
    return vmem_call(
        functools.partial(neck_kernel, head),
        [f32(rows, rows)],
        factor_scratch([], rows, rows)[1:],
        idx,
        [started],
        cost=60,
    )[0]


def tail_factor(top, second, chips, cuts, idx, head, order):
    rows = order - head * BLOCK
    return vmem_call(
        functools.partial(tail_kernel, chips, cuts, head, order),
        [f32(rows, order)],
        factor_scratch(lower_blocks(head, order // BLOCK), rows, order),
        idx,
        [top, *second],
        cost=25,
    )[0]


def apply_kernel(parts, head, idx_ref, top_ref, bottom_ref, *refs):
    pieces, outs = refs[:parts], refs[parts : 2 * parts]
    high_ref, low_ref, out_ref = refs[2 * parts :]
    rows = pieces[0].shape[0]
    order = rows * parts
    base = head * BLOCK
    for d in range(parts):
        at = pl.ds(pl.multiple_of(jnp.bitwise_xor(idx_ref[0], d) * rows, rows), rows)
        high_ref[at, :], low_ref[at, :] = halves(pieces[d][...])
    wide = 2 * BLOCK
    for r in range(0, order, wide):
        k = r + wide
        x = top_ref[r:k, :k] if k <= base else bottom_ref[r - base : k - base, :k]
        x_high, x_low = halves(x)
        out_ref[r:k, :] = mm(x_high, high_ref[:k, :]) + mm(x_high, low_ref[:k, :]) + mm(x_low, high_ref[:k, :])
    for d in range(parts):
        at = pl.ds(pl.multiple_of(jnp.bitwise_xor(idx_ref[0], d) * rows, rows), rows)
        outs[d][...] = out_ref[at, :]


def apply(top, bottom, pieces, idx, head):
    parts = len(pieces)
    rows, width = pieces[0].shape
    order = rows * parts
    return vmem_call(
        functools.partial(apply_kernel, parts, head),
        [f32(rows, width)] * parts,
        [
            pltpu.VMEM((order, width), jnp.bfloat16),
            pltpu.VMEM((order, width), jnp.bfloat16),
            pltpu.VMEM((order, width), jnp.float32),
        ],
        idx,
        [top, bottom] + list(pieces),
    )


def local(coeffs):
    band_rows, width = coeffs.shape
    parts = lax.axis_size("band")
    order = band_rows * parts
    columns_all = width * lax.axis_size("ga")
    head = order // BLOCK // 2
    band = lax.axis_index("band")
    idx = jnp.stack([band, band // 2, lax.axis_index("ga")]).astype(jnp.int32)
    pieces = cut_columns(coeffs, idx, parts)
    pieces = [pieces[0]] + [swap(pieces[d], "band", d) for d in range(1, parts)]
    keep1, send1, keep2, send2 = gram(pieces, idx, columns_all, head)
    cuts = lax.axis_size("ga") if lax.axis_size("ga") <= 4 else 1
    first, marks = sum_first(keep1, send1, idx)
    second = sum_second(keep2, send2, marks, idx)
    second = gather_ga(second, first)
    started = head_factor(first, parts, idx, head)
    second = gather_chips(second, started)
    top = neck_factor(started, idx, head)
    second = after(second, top)
    bottom = tail_factor(
        top, (second, swap(second, "band", 1)), parts // 2, cuts, idx, head, order
    )
    result = apply(top, bottom, pieces, idx, head)
    result = [result[0]] + [swap(result[d], "band", d) for d in range(1, parts)]
    return join_columns(result, idx)


def solution(mesh):
    return jax.shard_map(
        local,
        mesh=mesh,
        in_specs=(P("band", "ga"),),
        out_specs=P("band", "ga"),
        check_vma=False,
    )
```

profile of v0, /device:TPU:0, one launch (start us, length us, event | category | flops | bytes accessed | tf_op | source)
XLA Modules:
  0.0 156.3 jit_solution(1822100069141566881)
XLA Ops:
  0.1 1.6 %copy-done.16 = f32[128,4096]{1,0:T(8,128)S(1)} copy-done((f32[128,4096]{1,0:T(8,128)S(1)}, f32[128,4096]{1,0:T(8,128)}, u32[]{:S(2)}) %copy-start.16) | copy-done | bytes 2097176
  2.9 2.6 %collective-permute-start.1 = (f32[128,512]{1,0:T(8,128)S(1)}, f32[128,512]{1,0:T(8,128)S(1)}, u32[]{:S(2)}, u32[]{:S(2)}) collective-permute-start(f32[128,512]{1,0:T(8,128)S(1)} %get-tuple-element.49), channel_id=1, source_target_pairs={{0,8},{4,12},{8,0},{12,4},{16,24},{20,28},{24,16},{28,20},{1,9},{5... | collective-permute-start | bytes 786440 | tf_op jit(solution)/shard_map/ppermute | solution.py:249
  5.5 1.8 %collective-permute-start.3 = (f32[128,512]{1,0:T(8,128)S(1)}, f32[128,512]{1,0:T(8,128)S(1)}, u32[]{:S(2)}, u32[]{:S(2)}) collective-permute-start(f32[128,512]{1,0:T(8,128)S(1)} %get-tuple-element.51), channel_id=1, source_target_pairs={{0,16},{4,20},{8,24},{12,28},{16,0},{20,4},{24,8},{28,12},{1,17},{... | collective-permute-start | bytes 786440 | tf_op jit(solution)/shard_map/ppermute | solution.py:249
  7.3 2.6 %collective-permute-start.5 = (f32[128,512]{1,0:T(8,128)S(1)}, f32[128,512]{1,0:T(8,128)S(1)}, u32[]{:S(2)}, u32[]{:S(2)}) collective-permute-start(f32[128,512]{1,0:T(8,128)S(1)} %get-tuple-element.53), channel_id=1, source_target_pairs={{0,24},{4,28},{8,16},{12,20},{16,8},{20,12},{24,0},{28,4},{1,25},{... | collective-permute-start | bytes 786440 | tf_op jit(solution)/shard_map/ppermute | solution.py:249
  9.9 2.7 %collective-permute-done.1.refs_2_ = f32[128,512]{1,0:T(8,128)S(1)} collective-permute-done((f32[128,512]{1,0:T(8,128)S(1)}, f32[128,512]{1,0:T(8,128)S(1)}, u32[]{:S(2)}, u32[]{:S(2)}) %collective-permute-start.1) | collective-permute-done | bytes 262176 | tf_op jit(solution)/shard_map/ppermute | solution.py:249
  12.6 1.7 %collective-permute-start.6 = (f32[128,512]{1,0:T(8,128)S(1)}, f32[128,512]{1,0:T(8,128)S(1)}, u32[]{:S(2)}, u32[]{:S(2)}) collective-permute-start(f32[128,512]{1,0:T(8,128)S(1)} %get-tuple-element.54), channel_id=1, source_target_pairs={{0,28},{4,24},{8,20},{12,16},{16,12},{20,8},{24,4},{28,0},{1,29},{... | collective-permute-start | bytes 786440 | tf_op jit(solution)/shard_map/ppermute | solution.py:249
  14.3 3.4 %collective-permute-done.2.refs_3_ = f32[128,512]{1,0:T(8,128)S(1)} collective-permute-done((f32[128,512]{1,0:T(8,128)S(1)}, f32[128,512]{1,0:T(8,128)S(1)}, u32[]{:S(2)}, u32[]{:S(2)}) %collective-permute-start.2) | collective-permute-done | bytes 262176 | tf_op jit(solution)/shard_map/ppermute | solution.py:249
  17.7 12.5 %collective-permute-done.4.refs_5_ = f32[128,512]{1,0:T(8,128)S(1)} collective-permute-done((f32[128,512]{1,0:T(8,128)S(1)}, f32[128,512]{1,0:T(8,128)S(1)}, u32[]{:S(2)}, u32[]{:S(2)}) %collective-permute-start.4) | collective-permute-done | bytes 262176 | tf_op jit(solution)/shard_map/ppermute | solution.py:249
  30.2 3.9 %shard_map.18 = (f32[640,128]{1,0:T(8,128)S(1)}, f32[640,128]{1,0:T(8,128)S(1)}, f32[1664,128]{1,0:T(8,128)S(1)}, f32[1664,128]{1,0:T(8,128)S(1)}) custom-call(s32[3]{0:T(128)S(1)} %pad_add_fusion.idx_ref, f32[128,512]{1,0:T(8,128)S(1)} %get-tuple-element.47.refs_0_, f32[128,512]{1,0:T(8,128)S(1)} %collective-permute-done.refs_1_, ...), custom_call_target="tpu_custom_call" | custom-call | flops 1000000000 | tf_op jit(solution)/shard_map/pallas_call | solution.py:123
  37.7 1.7 %collective-permute-start.8 = (f32[160,128]{1,0:T(8,128)S(1)}, f32[160,128]{1,0:T(8,128)S(1)}, u32[]{:S(2)}, u32[]{:S(2)}) collective-permute-start(f32[160,128]{1,0:T(8,128)S(1)} %get-tuple-element.58), channel_id=1, source_target_pairs={{0,8},{4,12},{8,0},{12,4},{16,24},{20,28},{24,16},{28,20},{1,9},{5... | collective-permute-start | bytes 245768 | tf_op jit(solution)/shard_map/ppermute | solution.py:249
  39.4 1.5 collective-permute-start.9
  42.2 2.5 %collective-permute-done.9 = f32[160,128]{1,0:T(8,128)S(1)} collective-permute-done((f32[160,128]{1,0:T(8,128)S(1)}, f32[160,128]{1,0:T(8,128)S(1)}, u32[]{:S(2)}, u32[]{:S(2)}) %collective-permute-start.9) | collective-permute-done | bytes 81952 | tf_op jit(solution)/shard_map/ppermute | solution.py:249
  44.7 1.6 %collective-permute-done.10 = f32[160,128]{1,0:T(8,128)S(1)} collective-permute-done((f32[160,128]{1,0:T(8,128)S(1)}, f32[160,128]{1,0:T(8,128)S(1)}, u32[]{:S(2)}, u32[]{:S(2)}) %collective-permute-start.10) | collective-permute-done | bytes 81952 | tf_op jit(solution)/shard_map/ppermute | solution.py:249
  46.3 3.7 %collective-permute-start.13 = (f32[160,128]{1,0:T(8,128)S(1)}, f32[160,128]{1,0:T(8,128)S(1)}, u32[]{:S(2)}, u32[]{:S(2)}) collective-permute-start(f32[160,128]{1,0:T(8,128)S(1)} %add_add_fusion.1), channel_id=1, source_target_pairs={{0,3},{1,2},{2,1},{3,0},{4,7},{5,6},{6,5},{7,4},{8,11},{9,10},{10,... | collective-permute-start | bytes 245768 | tf_op jit(solution)/shard_map/ppermute | solution.py:249
  53.5 1.5 collective-permute-start.15
  55.9 3.8 %collective-permute-done.17.refs_3_ = f32[416,128]{1,0:T(8,128)S(1)} collective-permute-done((f32[416,128]{1,0:T(8,128)S(1)}, f32[416,128]{1,0:T(8,128)S(1)}, u32[]{:S(2)}, u32[]{:S(2)}) %collective-permute-start.17) | collective-permute-done | bytes 213024 | tf_op jit(solution)/shard_map/ppermute | solution.py:249
  59.7 1.8 %collective-permute-done.16.refs_2_ = f32[416,128]{1,0:T(8,128)S(1)} collective-permute-done((f32[416,128]{1,0:T(8,128)S(1)}, f32[416,128]{1,0:T(8,128)S(1)}, u32[]{:S(2)}, u32[]{:S(2)}) %collective-permute-start.16) | collective-permute-done | bytes 213024 | tf_op jit(solution)/shard_map/ppermute | solution.py:249
  62.1 3.5 %collective-permute-start.20 = (f32[104,128]{1,0:T(8,128)S(1)}, f32[104,128]{1,0:T(8,128)S(1)}, u32[]{:S(2)}, u32[]{:S(2)}) collective-permute-start(f32[104,128]{1,0:T(8,128)S(1)} %get-tuple-element.77), channel_id=1, source_target_pairs={{0,3},{1,2},{2,1},{3,0},{4,7},{5,6},{6,5},{7,4},{8,11},{9,10},{10,... | collective-permute-start | bytes 159752 | tf_op jit(solution)/shard_map/ppermute | solution.py:249
  66.6 9.8 %all_gather.3.first_ref = f32[1280,128]{1,0:T(8,128)S(1)} all-gather(f32[160,128]{1,0:T(8,128)S(1)} %add_add_fusion), channel_id=1, replica_groups=mesh['band'=8,'ga'=4] {'band'}, dimensions={0}, use_global_device_ids=true | all-gather | bytes 737280 | tf_op jit(solution)/shard_map/all_gather | solution.py:268
  76.4 3.5 %collective-permute-start.23 = (f32[104,128]{1,0:T(8,128)S(1)}, f32[104,128]{1,0:T(8,128)S(1)}, u32[]{:S(2)}, u32[]{:S(2)}) collective-permute-start(f32[104,128]{1,0:T(8,128)S(1)} %add_add_fusion.2), channel_id=1, source_target_pairs={{0,3},{1,2},{2,1},{3,0},{4,7},{5,6},{6,5},{7,4},{8,11},{9,10},{10,... | collective-permute-start | bytes 159752 | tf_op jit(solution)/shard_map/ppermute | solution.py:249
  80.9 7.6 %shard_map.20.in_ref = f32[512,512]{1,0:T(8,128)S(1)} custom-call(s32[3]{0:T(128)S(1)} %pad_add_fusion.idx_ref, f32[1280,128]{1,0:T(8,128)S(1)} %all_gather.3.first_ref), custom_call_target="tpu_custom_call" | custom-call | flops 60000002048 | tf_op jit(solution)/shard_map/pallas_call | solution.py:123
  89.5 3.7 %all-to-all-start = ((f32[4,416,128]{2,1,0:T(8,128)}), f32[4,416,128]{2,1,0:T(8,128)S(1)}, u32[]{:S(2)}, u32[]{:S(2)}) async-start(f32[4,416,128]{2,1,0:T(8,128)} %broadcast_in_dim.3), calls=%async_computation | async-start | bytes 1703936 | tf_op jit(solution)/shard_map/all_to_all | solution.py:296
  93.2 6.9 %shard_map.21.top_ref = f32[512,512]{1,0:T(8,128)S(1)} custom-call(s32[3]{0:T(128)S(1)} %pad_add_fusion.idx_ref, f32[512,512]{1,0:T(8,128)S(1)} %shard_map.20.in_ref), custom_call_target="tpu_custom_call" | custom-call | flops 60000002048 | tf_op jit(solution)/shard_map/pallas_call | solution.py:123
  100.1 4.3 %all-to-all-done = f32[4,416,128]{2,1,0:T(8,128)S(1)} async-done(((f32[4,416,128]{2,1,0:T(8,128)}), f32[4,416,128]{2,1,0:T(8,128)S(1)}, u32[]{:S(2)}, u32[]{:S(2)}) %all-to-all-start) | async-done | bytes 852000 | tf_op jit(solution)/shard_map/all_to_all | solution.py:296
  104.6 2.4 %collective-permute-done.24.far_ref = f32[1664,128]{1,0:T(8,128)S(1)} collective-permute-done((f32[1664,128]{1,0:T(8,128)S(1)}, f32[1664,128]{1,0:T(8,128)S(1)}, u32[]{:S(2)}, u32[]{:S(2)}) %collective-permute-start.24) | collective-permute-done | bytes 852000 | tf_op jit(solution)/shard_map/ppermute | solution.py:249
  106.9 16.9 %shard_map.24.bottom_ref = f32[512,1024]{1,0:T(8,128)S(1)} custom-call(s32[3]{0:T(128)S(1)} %pad_add_fusion.idx_ref, f32[512,512]{1,0:T(8,128)S(1)} %shard_map.21.top_ref, f32[1664,128]{1,0:T(8,128)S(1)} %bitcast.5, f32[1664,128]{1,0:T(8,128)S(1)} %collective-permute-done.24.far_ref), custom_call_target="tpu_custom_call" | custom-call | flops 24999999488 | tf_op jit(solution)/shard_map/pallas_call | solution.py:123
  123.9 3.4 %shard_map.25 = (f32[128,512]{1,0:T(8,128)S(1)}, f32[128,512]{1,0:T(8,128)S(1)}, f32[128,512]{1,0:T(8,128)S(1)}, f32[128,512]{1,0:T(8,128)S(1)}, f32[128,512]{1,...) custom-call(s32[3]{0:T(128)S(1)} %pad_add_fusion.idx_ref, ...), custom_call_target="tpu_custom_call" | custom-call | flops 1000000000 | tf_op jit(solution)/shard_map/pallas_call | solution.py:123
  129.2 1.5 collective-permute-start.28
  132.4 4.2 %collective-permute-done.26.refs_2_ = f32[128,512]{1,0:T(8,128)S(1)} collective-permute-done((f32[128,512]{1,0:T(8,128)S(1)}, f32[128,512]{1,0:T(8,128)S(1)}, u32[]{:S(2)}, u32[]{:S(2)}) %collective-permute-start.26) | collective-permute-done | bytes 262176 | tf_op jit(solution)/shard_map/ppermute | solution.py:249
  136.7 4.5 %collective-permute-done.27.refs_3_ = f32[128,512]{1,0:T(8,128)S(1)} collective-permute-done((f32[128,512]{1,0:T(8,128)S(1)}, f32[128,512]{1,0:T(8,128)S(1)}, u32[]{:S(2)}, u32[]{:S(2)}) %collective-permute-start.27) | collective-permute-done | bytes 262176 | tf_op jit(solution)/shard_map/ppermute | solution.py:249
  141.2 13.1 %collective-permute-done.29.refs_5_ = f32[128,512]{1,0:T(8,128)S(1)} collective-permute-done((f32[128,512]{1,0:T(8,128)S(1)}, f32[128,512]{1,0:T(8,128)S(1)}, u32[]{:S(2)}, u32[]{:S(2)}) %collective-permute-start.29) | collective-permute-done | bytes 262176 | tf_op jit(solution)/shard_map/ppermute | solution.py:249
  154.3 2.0 %shard_map.26 = f32[128,4096]{1,0:T(8,128)} custom-call(s32[3]{0:T(128)S(1)} %pad_add_fusion.idx_ref, f32[128,512]{1,0:T(8,128)S(1)} %get-tuple-element.81.refs_0_, f32[128,512]{1,0:T(8,128)S(1)} %collective-permute-done.25.refs_1_, f32[128,512]{1,0:T(8,128)S(1)} %collective-permute-done.26.refs_2_, f32[128,512]{1,0:T(8,128)S(1)} %collective-permute-done.27.refs_3_, ...), custom_call_target="tpu_custom_call" | custom-call | flops 1000000000 | tf_op jit(solution)/shard_map/pallas_call | solution.py:123
  (85 shorter events, 17.9 us)
Async XLA Ops:
  2.4 4.9 %collective-permute-start = (f32[128,512]{1,0:T(8,128)S(1)}, f32[128,512]{1,0:T(8,128)S(1)}, u32[]{:S(2)}, u32[]{:S(2)}) collective-permute-start(f32[128,512]{1,0:T(8,128)S(1)} %get-tuple-element.48), channel_id=1, source_target_pairs={{0,4},{4,0},{8,12},{12,8},{16,20},{20,16},{24,28},{28,24},{1,5},{5... | collective-permute-start | bytes 786440 | tf_op jit(solution)/shard_map/ppermute | solution.py:249
  2.9 9.7 %collective-permute-start.1 = (f32[128,512]{1,0:T(8,128)S(1)}, f32[128,512]{1,0:T(8,128)S(1)}, u32[]{:S(2)}, u32[]{:S(2)}) collective-permute-start(f32[128,512]{1,0:T(8,128)S(1)} %get-tuple-element.49), channel_id=1, source_target_pairs={{0,8},{4,12},{8,0},{12,4},{16,24},{20,28},{24,16},{28,20},{1,9},{5... | collective-permute-start | bytes 786440 | tf_op jit(solution)/shard_map/ppermute | solution.py:249
  5.5 12.3 %collective-permute-start.2 = (f32[128,512]{1,0:T(8,128)S(1)}, f32[128,512]{1,0:T(8,128)S(1)}, u32[]{:S(2)}, u32[]{:S(2)}) collective-permute-start(f32[128,512]{1,0:T(8,128)S(1)} %get-tuple-element.50), channel_id=1, source_target_pairs={{0,12},{4,8},{8,4},{12,0},{16,28},{20,24},{24,20},{28,16},{1,13},{... | collective-permute-start | bytes 786440 | tf_op jit(solution)/shard_map/ppermute | solution.py:249
  5.5 12.2 %collective-permute-start.3 = (f32[128,512]{1,0:T(8,128)S(1)}, f32[128,512]{1,0:T(8,128)S(1)}, u32[]{:S(2)}, u32[]{:S(2)}) collective-permute-start(f32[128,512]{1,0:T(8,128)S(1)} %get-tuple-element.51), channel_id=1, source_target_pairs={{0,16},{4,20},{8,24},{12,28},{16,0},{20,4},{24,8},{28,12},{1,17},{... | collective-permute-start | bytes 786440 | tf_op jit(solution)/shard_map/ppermute | solution.py:249
  7.3 22.9 %collective-permute-start.4 = (f32[128,512]{1,0:T(8,128)S(1)}, f32[128,512]{1,0:T(8,128)S(1)}, u32[]{:S(2)}, u32[]{:S(2)}) collective-permute-start(f32[128,512]{1,0:T(8,128)S(1)} %get-tuple-element.52), channel_id=1, source_target_pairs={{0,20},{4,16},{8,28},{12,24},{16,4},{20,0},{24,12},{28,8},{1,21},{... | collective-permute-start | bytes 786440 | tf_op jit(solution)/shard_map/ppermute | solution.py:249
  7.3 22.9 %collective-permute-start.5 = (f32[128,512]{1,0:T(8,128)S(1)}, f32[128,512]{1,0:T(8,128)S(1)}, u32[]{:S(2)}, u32[]{:S(2)}) collective-permute-start(f32[128,512]{1,0:T(8,128)S(1)} %get-tuple-element.53), channel_id=1, source_target_pairs={{0,24},{4,28},{8,16},{12,20},{16,8},{20,12},{24,0},{28,4},{1,25},{... | collective-permute-start | bytes 786440 | tf_op jit(solution)/shard_map/ppermute | solution.py:249
  12.6 17.6 %collective-permute-start.6 = (f32[128,512]{1,0:T(8,128)S(1)}, f32[128,512]{1,0:T(8,128)S(1)}, u32[]{:S(2)}, u32[]{:S(2)}) collective-permute-start(f32[128,512]{1,0:T(8,128)S(1)} %get-tuple-element.54), channel_id=1, source_target_pairs={{0,28},{4,24},{8,20},{12,16},{16,12},{20,8},{24,4},{28,0},{1,29},{... | collective-permute-start | bytes 786440 | tf_op jit(solution)/shard_map/ppermute | solution.py:249
  37.3 13.5 %collective-permute-start.14 = (f32[1664,128]{1,0:T(8,128)S(1)}, f32[1664,128]{1,0:T(8,128)S(1)}, u32[]{:S(2)}, u32[]{:S(2)}) collective-permute-start(f32[1664,128]{1,0:T(8,128)S(1)} %get-tuple-element.63), channel_id=1, source_target_pairs={{0,4},{4,0},{8,12},{12,8},{16,20},{20,16},{24,28},{28,24},{1,5},{5... | collective-permute-start | bytes 2555912 | tf_op jit(solution)/shard_map/ppermute | solution.py:249
  37.7 4.5 %collective-permute-start.8 = (f32[160,128]{1,0:T(8,128)S(1)}, f32[160,128]{1,0:T(8,128)S(1)}, u32[]{:S(2)}, u32[]{:S(2)}) collective-permute-start(f32[160,128]{1,0:T(8,128)S(1)} %get-tuple-element.58), channel_id=1, source_target_pairs={{0,8},{4,12},{8,0},{12,4},{16,24},{20,28},{24,16},{28,20},{1,9},{5... | collective-permute-start | bytes 245768 | tf_op jit(solution)/shard_map/ppermute | solution.py:249
  39.4 5.3 %collective-permute-start.9 = (f32[160,128]{1,0:T(8,128)S(1)}, f32[160,128]{1,0:T(8,128)S(1)}, u32[]{:S(2)}, u32[]{:S(2)}) collective-permute-start(f32[160,128]{1,0:T(8,128)S(1)} %get-tuple-element.59), channel_id=1, source_target_pairs={{0,16},{4,20},{8,24},{12,28},{16,0},{20,4},{24,8},{28,12},{1,17},{... | collective-permute-start | bytes 245768 | tf_op jit(solution)/shard_map/ppermute | solution.py:249
  41.0 5.3 %collective-permute-start.10 = (f32[160,128]{1,0:T(8,128)S(1)}, f32[160,128]{1,0:T(8,128)S(1)}, u32[]{:S(2)}, u32[]{:S(2)}) collective-permute-start(f32[160,128]{1,0:T(8,128)S(1)} %get-tuple-element.60), channel_id=1, source_target_pairs={{0,24},{4,28},{8,16},{12,20},{16,8},{20,12},{24,0},{28,4},{1,25},{... | collective-permute-start | bytes 245768 | tf_op jit(solution)/shard_map/ppermute | solution.py:249
  46.3 7.2 %collective-permute-start.13 = (f32[160,128]{1,0:T(8,128)S(1)}, f32[160,128]{1,0:T(8,128)S(1)}, u32[]{:S(2)}, u32[]{:S(2)}) collective-permute-start(f32[160,128]{1,0:T(8,128)S(1)} %add_add_fusion.1), channel_id=1, source_target_pairs={{0,3},{1,2},{2,1},{3,0},{4,7},{5,6},{6,5},{7,4},{8,11},{9,10},{10,... | collective-permute-start | bytes 245768 | tf_op jit(solution)/shard_map/ppermute | solution.py:249
  50.0 5.9 %collective-permute-start.12 = (f32[160,128]{1,0:T(8,128)S(1)}, f32[160,128]{1,0:T(8,128)S(1)}, u32[]{:S(2)}, u32[]{:S(2)}) collective-permute-start(f32[160,128]{1,0:T(8,128)S(1)} %add_add_fusion.1), channel_id=1, source_target_pairs={{0,2},{1,3},{2,0},{3,1},{4,6},{5,7},{6,4},{7,5},{8,10},{9,11},{10,... | collective-permute-start | bytes 245768 | tf_op jit(solution)/shard_map/ppermute | solution.py:249
  50.0 5.9 %collective-permute-start.11 = (f32[160,128]{1,0:T(8,128)S(1)}, f32[160,128]{1,0:T(8,128)S(1)}, u32[]{:S(2)}, u32[]{:S(2)}) collective-permute-start(f32[160,128]{1,0:T(8,128)S(1)} %add_add_fusion.1), channel_id=1, source_target_pairs={{0,1},{1,0},{2,3},{3,2},{4,5},{5,4},{6,7},{7,6},{8,9},{9,8},{10,11... | collective-permute-start | bytes 245768 | tf_op jit(solution)/shard_map/ppermute | solution.py:249
  51.4 8.3 %collective-permute-start.17 = (f32[416,128]{1,0:T(8,128)S(1)}, f32[416,128]{1,0:T(8,128)S(1)}, u32[]{:S(2)}, u32[]{:S(2)}) collective-permute-start(f32[416,128]{1,0:T(8,128)S(1)} %get-tuple-element.70), channel_id=1, source_target_pairs={{0,24},{4,28},{8,16},{12,20},{16,8},{20,12},{24,0},{28,4},{1,25},{... | collective-permute-start | bytes 638984 | tf_op jit(solution)/shard_map/ppermute | solution.py:249
  52.2 9.3 %collective-permute-start.16 = (f32[416,128]{1,0:T(8,128)S(1)}, f32[416,128]{1,0:T(8,128)S(1)}, u32[]{:S(2)}, u32[]{:S(2)}) collective-permute-start(f32[416,128]{1,0:T(8,128)S(1)} %get-tuple-element.68), channel_id=1, source_target_pairs={{0,16},{4,20},{8,24},{12,28},{16,0},{20,4},{24,8},{28,12},{1,17},{... | collective-permute-start | bytes 638984 | tf_op jit(solution)/shard_map/ppermute | solution.py:249
  53.5 8.0 %collective-permute-start.15 = (f32[416,128]{1,0:T(8,128)S(1)}, f32[416,128]{1,0:T(8,128)S(1)}, u32[]{:S(2)}, u32[]{:S(2)}) collective-permute-start(f32[416,128]{1,0:T(8,128)S(1)} %get-tuple-element.66), channel_id=1, source_target_pairs={{0,8},{4,12},{8,0},{12,4},{16,24},{20,28},{24,16},{28,20},{1,9},{5... | collective-permute-start | bytes 638984 | tf_op jit(solution)/shard_map/ppermute | solution.py:249
  62.1 14.2 %collective-permute-start.20 = (f32[104,128]{1,0:T(8,128)S(1)}, f32[104,128]{1,0:T(8,128)S(1)}, u32[]{:S(2)}, u32[]{:S(2)}) collective-permute-start(f32[104,128]{1,0:T(8,128)S(1)} %get-tuple-element.77), channel_id=1, source_target_pairs={{0,3},{1,2},{2,1},{3,0},{4,7},{5,6},{6,5},{7,4},{8,11},{9,10},{10,... | collective-permute-start | bytes 159752 | tf_op jit(solution)/shard_map/ppermute | solution.py:249
  65.6 10.7 %collective-permute-start.19 = (f32[104,128]{1,0:T(8,128)S(1)}, f32[104,128]{1,0:T(8,128)S(1)}, u32[]{:S(2)}, u32[]{:S(2)}) collective-permute-start(f32[104,128]{1,0:T(8,128)S(1)} %get-tuple-element.75), channel_id=1, source_target_pairs={{0,2},{1,3},{2,0},{3,1},{4,6},{5,7},{6,4},{7,5},{8,10},{9,11},{10,... | collective-permute-start | bytes 159752 | tf_op jit(solution)/shard_map/ppermute | solution.py:249
  65.6 10.7 %collective-permute-start.18 = (f32[104,128]{1,0:T(8,128)S(1)}, f32[104,128]{1,0:T(8,128)S(1)}, u32[]{:S(2)}, u32[]{:S(2)}) collective-permute-start(f32[104,128]{1,0:T(8,128)S(1)} %get-tuple-element.73), channel_id=1, source_target_pairs={{0,1},{1,0},{2,3},{3,2},{4,5},{5,4},{6,7},{7,6},{8,9},{9,8},{10,11... | collective-permute-start | bytes 159752 | tf_op jit(solution)/shard_map/ppermute | solution.py:249
  76.4 12.1 %collective-permute-start.23 = (f32[104,128]{1,0:T(8,128)S(1)}, f32[104,128]{1,0:T(8,128)S(1)}, u32[]{:S(2)}, u32[]{:S(2)}) collective-permute-start(f32[104,128]{1,0:T(8,128)S(1)} %add_add_fusion.2), channel_id=1, source_target_pairs={{0,3},{1,2},{2,1},{3,0},{4,7},{5,6},{6,5},{7,4},{8,11},{9,10},{10,... | collective-permute-start | bytes 159752 | tf_op jit(solution)/shard_map/ppermute | solution.py:249
  79.9 8.6 %collective-permute-start.22 = (f32[104,128]{1,0:T(8,128)S(1)}, f32[104,128]{1,0:T(8,128)S(1)}, u32[]{:S(2)}, u32[]{:S(2)}) collective-permute-start(f32[104,128]{1,0:T(8,128)S(1)} %add_add_fusion.2), channel_id=1, source_target_pairs={{0,2},{1,3},{2,0},{3,1},{4,6},{5,7},{6,4},{7,5},{8,10},{9,11},{10,... | collective-permute-start | bytes 159752 | tf_op jit(solution)/shard_map/ppermute | solution.py:249
  79.9 8.6 %collective-permute-start.21 = (f32[104,128]{1,0:T(8,128)S(1)}, f32[104,128]{1,0:T(8,128)S(1)}, u32[]{:S(2)}, u32[]{:S(2)}) collective-permute-start(f32[104,128]{1,0:T(8,128)S(1)} %add_add_fusion.2), channel_id=1, source_target_pairs={{0,1},{1,0},{2,3},{3,2},{4,5},{5,4},{6,7},{7,6},{8,9},{9,8},{10,11... | collective-permute-start | bytes 159752 | tf_op jit(solution)/shard_map/ppermute | solution.py:249
  89.5 15.0 %all-to-all-start = ((f32[4,416,128]{2,1,0:T(8,128)}), f32[4,416,128]{2,1,0:T(8,128)S(1)}, u32[]{:S(2)}, u32[]{:S(2)}) async-start(f32[4,416,128]{2,1,0:T(8,128)} %broadcast_in_dim.3), calls=%async_computation | async-start | bytes 1703936 | tf_op jit(solution)/shard_map/all_to_all | solution.py:296
  104.5 2.4 %collective-permute-start.24 = (f32[1664,128]{1,0:T(8,128)S(1)}, f32[1664,128]{1,0:T(8,128)S(1)}, u32[]{:S(2)}, u32[]{:S(2)}) collective-permute-start(f32[1664,128]{1,0:T(8,128)S(1)} %bitcast.4), channel_id=1, source_target_pairs={{0,4},{4,0},{8,12},{12,8},{16,20},{20,16},{24,28},{28,24},{1,5},{5... | collective-permute-start | bytes 2555912 | tf_op jit(solution)/shard_map/ppermute | solution.py:249
  127.3 3.7 %collective-permute-start.25 = (f32[128,512]{1,0:T(8,128)S(1)}, f32[128,512]{1,0:T(8,128)S(1)}, u32[]{:S(2)}, u32[]{:S(2)}) collective-permute-start(f32[128,512]{1,0:T(8,128)S(1)} %get-tuple-element.82), channel_id=1, source_target_pairs={{0,4},{4,0},{8,12},{12,8},{16,20},{20,16},{24,28},{28,24},{1,5},{5... | collective-permute-start | bytes 786440 | tf_op jit(solution)/shard_map/ppermute | solution.py:249
  127.5 9.1 %collective-permute-start.26 = (f32[128,512]{1,0:T(8,128)S(1)}, f32[128,512]{1,0:T(8,128)S(1)}, u32[]{:S(2)}, u32[]{:S(2)}) collective-permute-start(f32[128,512]{1,0:T(8,128)S(1)} %get-tuple-element.83), channel_id=1, source_target_pairs={{0,8},{4,12},{8,0},{12,4},{16,24},{20,28},{24,16},{28,20},{1,9},{5... | collective-permute-start | bytes 786440 | tf_op jit(solution)/shard_map/ppermute | solution.py:249
  128.9 12.3 %collective-permute-start.27 = (f32[128,512]{1,0:T(8,128)S(1)}, f32[128,512]{1,0:T(8,128)S(1)}, u32[]{:S(2)}, u32[]{:S(2)}) collective-permute-start(f32[128,512]{1,0:T(8,128)S(1)} %get-tuple-element.84), channel_id=1, source_target_pairs={{0,12},{4,8},{8,4},{12,0},{16,28},{20,24},{24,20},{28,16},{1,13},{... | collective-permute-start | bytes 786440 | tf_op jit(solution)/shard_map/ppermute | solution.py:249
  129.2 12.0 %collective-permute-start.28 = (f32[128,512]{1,0:T(8,128)S(1)}, f32[128,512]{1,0:T(8,128)S(1)}, u32[]{:S(2)}, u32[]{:S(2)}) collective-permute-start(f32[128,512]{1,0:T(8,128)S(1)} %get-tuple-element.85), channel_id=1, source_target_pairs={{0,16},{4,20},{8,24},{12,28},{16,0},{20,4},{24,8},{28,12},{1,17},{... | collective-permute-start | bytes 786440 | tf_op jit(solution)/shard_map/ppermute | solution.py:249
  130.7 23.6 %collective-permute-start.29 = (f32[128,512]{1,0:T(8,128)S(1)}, f32[128,512]{1,0:T(8,128)S(1)}, u32[]{:S(2)}, u32[]{:S(2)}) collective-permute-start(f32[128,512]{1,0:T(8,128)S(1)} %get-tuple-element.86), channel_id=1, source_target_pairs={{0,20},{4,16},{8,28},{12,24},{16,4},{20,0},{24,12},{28,8},{1,21},{... | collective-permute-start | bytes 786440 | tf_op jit(solution)/shard_map/ppermute | solution.py:249
  131.0 23.2 %collective-permute-start.30 = (f32[128,512]{1,0:T(8,128)S(1)}, f32[128,512]{1,0:T(8,128)S(1)}, u32[]{:S(2)}, u32[]{:S(2)}) collective-permute-start(f32[128,512]{1,0:T(8,128)S(1)} %get-tuple-element.87), channel_id=1, source_target_pairs={{0,24},{4,28},{8,16},{12,20},{16,8},{20,12},{24,0},{28,4},{1,25},{... | collective-permute-start | bytes 786440 | tf_op jit(solution)/shard_map/ppermute | solution.py:249
  136.6 17.6 %collective-permute-start.31 = (f32[128,512]{1,0:T(8,128)S(1)}, f32[128,512]{1,0:T(8,128)S(1)}, u32[]{:S(2)}, u32[]{:S(2)}) collective-permute-start(f32[128,512]{1,0:T(8,128)S(1)} %get-tuple-element.88), channel_id=1, source_target_pairs={{0,28},{4,24},{8,20},{12,16},{16,12},{20,8},{24,4},{28,0},{1,29},{... | collective-permute-start | bytes 786440 | tf_op jit(solution)/shard_map/ppermute | solution.py:249
  (18 other events, 271.8 us)
where the time goes:
time: 156 us
  waiting for transfers between devices  59.9 us (38%)
  Pallas kernels  43.2 us (28%)
  starting transfers between devices  39.6 us (25%)
  blocking collectives  9.78 us (6%)
  local copies, waits for them, and re-layouts  3.3 us (2%)
    ppermute x32, waiting for transfers between devices, swap(): lax.ppermute(x, axis, [(i, i ^ d) for i in range(lax.axis_size(axis))])  55.6 us
    pallas_call x10, Pallas kernels, vmem_call(): pl.pallas_call(kernel, out_shape=shapes, in_specs=[pl.BlockSpec(memory_sp...  43.2 us
    ppermute x32, starting transfers between devices, swap(): lax.ppermute(x, axis, [(i, i ^ d) for i in range(lax.axis_size(axis))])  35.9 us
    all_gather x1, blocking collectives, sum_first(): lax.all_gather(total, 'band', axis=0, tiled=True)  9.78 us
    all_to_all x1, waiting for transfers between devices, gather_chips(): got = lax.all_to_all(copies, 'band', 0, 0, axis_index_groups=groups)  4.33 us
    all_to_all x1, starting transfers between devices, gather_chips(): got = lax.all_to_all(copies, 'band', 0, 0, axis_index_groups=groups)  3.68 us
  transfers between devices with their start and end apart: 33, of which 15 were waited for; matrix products, arithmetic and copies ran while one was open for 0% of the time, Pallas kernels for 10%

commit v1 on v0

v1 whole, which is shorter than its diff:
```python
import functools

import jax
import jax.numpy as jnp
from jax import lax
from jax.experimental import pallas as pl
from jax.experimental.pallas import tpu as pltpu
from jax.sharding import PartitionSpec as P

BLOCK = 128
STRIP = 8
NN = (((1,), (0,)), ((), ()))
NT = (((1,), (1,)), ((), ()))


def halves(x):
    high = x.astype(jnp.bfloat16)
    return high, (x - high.astype(jnp.float32)).astype(jnp.bfloat16)


def left3(x):
    high, low = halves(x)
    return jnp.concatenate([high, low, high], axis=1)


def right3(x):
    high, low = halves(x)
    return jnp.concatenate([high, high, low], axis=0)


def right3t(x):
    high, low = halves(x)
    return jnp.concatenate([high, high, low], axis=1)


def mm(a, b, dims=NN):
    return lax.dot_general(a, b, dims, preferred_element_type=jnp.float32)


NEAR = 2


def leaf(strips, row_ref, col_ref, pending):
    share = -(-len(pending) // (BLOCK // STRIP - 4))
    strips = list(strips)
    count = len(strips)
    shape = strips[0].shape
    lane = lax.broadcasted_iota(jnp.int32, shape, 1)
    sub = lax.broadcasted_iota(jnp.int32, shape, 0)
    each = range(STRIP)

    def column(x, c):
        return jnp.broadcast_to(x[:, c : c + 1], shape)

    def repeated(ref, r):
        return jnp.broadcast_to(ref[r : r + 1, :], shape)

    for s in range(count):
        base = STRIP * s
        row_ref[base : base + STRIP, :] = strips[s]
        for b in each:
            at = (base + b) * STRIP
            col_ref[at : at + STRIP, :] = column(strips[s], base + b)
        rows = [repeated(row_ref, base + q) for q in each]
        piv = [
            [repeated(col_ref, (base + b) * STRIP + a) if b >= a else None for b in each] for a in each
        ]
        panel = (lane >= base) & (lane < base + STRIP)
        rows = [jnp.where(panel, jnp.where(lane == base + q, 1.0, 0.0), rows[q]) for q in each]
        mult = [[None] * STRIP for _ in each]
        done = [None] * STRIP
        gain = [None] * STRIP
        for q in each:
            root = lax.rsqrt(piv[q][q])
            inv = root * root
            for a in range(q + 1, STRIP):
                mult[a][q] = piv[q][a] * inv
            for a in range(q + 1, STRIP):
                for b in range(a, STRIP):
                    piv[a][b] = piv[a][b] - mult[a][q] * piv[q][b]
                rows[a] = rows[a] - mult[a][q] * rows[q]
            gain[q] = rows[q] * inv
            done[q] = rows[q] * root
        for q in range(STRIP - 1, 0, -1):
            for a in range(q):
                gain[a] = gain[a] - mult[q][a] * gain[q]
        far = s + 1 + NEAR
        for t in range(s + 1, min(far, count)):
            terms = [column(strips[t], base + q) * gain[q] for q in each]
            while len(terms) > 1:
                terms = [terms[i] + terms[i + 1] for i in range(0, len(terms), 2)]
            strips[t] = jnp.where(panel, 0.0, strips[t]) - terms[0]
        if far < count:
            g = gain[0]
            for q in range(1, STRIP):
                g = jnp.where(sub == q, gain[q], g)
            below = STRIP * (count - s - 1)

            def padded(x):
                parts = [x]
                if base:
                    parts = [jnp.zeros((base, BLOCK), x.dtype)] + parts
                if below:
                    parts = parts + [jnp.zeros((below, BLOCK), x.dtype)]
                return jnp.concatenate(parts, axis=0)

            g_high, g_low = [padded(x) for x in halves(g)]
            s_high, s_low = halves(jnp.concatenate(strips[far:], axis=0))
            t = mm(
                jnp.concatenate([s_high, s_low], axis=1), jnp.concatenate([g_high, g_high], axis=0)
            ) + mm(s_high, g_low)
            for i in range(far, count):
                at = STRIP * (i - far)
                strips[i] = jnp.where(panel, 0.0, strips[i]) - t[at : at + STRIP, :]
        new = done[0]
        for q in range(1, STRIP):
            new = jnp.where(sub == q, done[q], new)
        strips[s] = new
        for _ in range(min(share, len(pending))):
            pending.pop(0)()
    return [jnp.where(lane <= sub + STRIP * s, strips[s], 0.0) for s in range(count)]


def vmem_call(kernel, shapes, scratch, idx, operands, cost=1, vmem=12):
    space = pl.BlockSpec(memory_space=pltpu.VMEM)
    return pl.pallas_call(
        kernel,
        out_shape=shapes,
        in_specs=[pl.BlockSpec(memory_space=pltpu.SMEM)] + [space] * len(operands),
        out_specs=[space] * len(shapes),
        scratch_shapes=scratch,
        compiler_params=pltpu.CompilerParams(vmem_limit_bytes=vmem * 2**20),
        cost_estimate=pl.CostEstimate(
            flops=cost * 1_000_000_000, bytes_accessed=0, transcendentals=0
        ),
    )(idx, *operands)


def f32(*shape):
    return jax.ShapeDtypeStruct(shape, jnp.float32)


def cut_columns(x, band, parts):
    width = x.shape[1] // parts
    return [lax.dynamic_slice_in_dim(x, (band ^ d) * width, width, 1) for d in range(parts)]


def join_kernel(parts, width, idx_ref, *refs):
    for d in range(parts):
        start = pl.multiple_of(jnp.bitwise_xor(idx_ref[0], d) * width, width)
        refs[parts][:, pl.ds(start, width)] = refs[d][...]


def join_columns(pieces, idx):
    parts = len(pieces)
    rows, width = pieces[0].shape
    return vmem_call(
        functools.partial(join_kernel, parts, width), [f32(rows, width * parts)], [], idx, pieces, vmem=8
    )[0]


def sum_split_kernel(terms, sections, parts, slot, idx_ref, *refs):
    ins, outs = refs[:terms], list(refs[terms:])
    first = 0
    for length in sections:
        rows = length // parts
        for d in range(parts):
            start = first + jnp.bitwise_xor(idx_ref[slot], d) * rows
            part = pl.ds(pl.multiple_of(start, 8), rows)
            total = ins[0][part, :]
            for r in ins[1:]:
                total = total + r[part, :]
            outs.pop(0)[...] = total
        first += length


def sum_split(terms, sections, parts, slot, idx):
    width = terms[0].shape[1]
    cut = vmem_call(
        functools.partial(sum_split_kernel, len(terms), sections, parts, slot),
        [f32(length // parts, width) for length in sections for _ in range(parts)],
        [],
        idx,
        terms,
    )
    return [cut[n * parts : (n + 1) * parts] for n in range(len(sections))]


def lower_blocks(first, last):
    return [(i, j) for i in range(first, last) for j in range(i + 1)]


def mm3(a_high, a_low, b_high, b_low, dims=NN):
    return mm(a_high, b_high, dims) + mm(a_high, b_low, dims) + mm(a_low, b_high, dims)


def gram_kernel(parts, scale, head, order, idx_ref, *refs):
    pieces = refs[:parts]
    keep_ref, send_ref, high_ref, low_ref, flat_ref = refs[parts:]
    rows = pieces[0].shape[0]
    for d in range(parts):
        at = pl.ds(pl.multiple_of(jnp.bitwise_xor(idx_ref[0], d) * rows, rows), rows)
        high_ref[at, :], low_ref[at, :] = halves(pieces[d][...])
    place = {}
    first = 0
    for blocks in (lower_blocks(0, head), lower_blocks(head, order // BLOCK)):
        half = len(blocks) // 2
        for n, block in enumerate(blocks):
            place[block] = (n // half, first + n % half * BLOCK)
        first += half * BLOCK
    wide = 2 * BLOCK
    for c in range(0, order, wide):
        t = scale * mm3(
            high_ref[c:, :], low_ref[c:, :], high_ref[c : c + wide, :], low_ref[c : c + wide, :], NT
        )
        for i in range(c // BLOCK, order // BLOCK):
            for j in (c // BLOCK, c // BLOCK + 1):
                if j <= i:
                    half, row = place[i, j]
                    flat_ref[half, row : row + BLOCK, :] = t[
                        i * BLOCK - c : (i + 1) * BLOCK - c, j * BLOCK - c : (j + 1) * BLOCK - c
                    ]
    core = jnp.bitwise_and(idx_ref[0], 1)
    keep_ref[...] = flat_ref[core]
    send_ref[...] = flat_ref[1 - core]


def gram(pieces, idx, columns_all, head):
    parts = len(pieces)
    rows, width = pieces[0].shape
    order = rows * parts
    length = len(lower_blocks(0, order // BLOCK)) * BLOCK // 2
    term = jax.ShapeDtypeStruct((order, width), jnp.bfloat16)
    return vmem_call(
        functools.partial(gram_kernel, parts, 1.0 / columns_all, head, order),
        [f32(length, BLOCK), f32(length, BLOCK), term, term],
        [pltpu.VMEM((2, length, BLOCK), jnp.float32)],
        idx,
        pieces,
        vmem=20,
    )


def swap(x, axis, d):
    return lax.ppermute(x, axis, [(i, i ^ d) for i in range(lax.axis_size(axis))])


def sum_all(terms):
    return sum(terms[1:], terms[0])


def sum_band(keep, send, head, order, idx):
    chips = lax.axis_size("band") // 2
    sections = [
        len(blocks) * BLOCK // 2 for blocks in (lower_blocks(0, head), lower_blocks(head, order // BLOCK))
    ]
    return sum_split([keep, swap(send, "band", 1)], sections, chips, 1, idx)


def sum_chips(pieces):
    return [pieces[0]] + [swap(pieces[d], "band", 2 * d) for d in range(1, len(pieces))]


def sum_first(terms):
    depth = lax.axis_size("ga")
    part = sum_all(terms)
    if depth <= 4:
        total = sum_all([part] + [swap(part, "ga", d) for d in range(1, depth)])
    else:
        total = lax.psum(part, "ga")
    return lax.all_gather(total, "band", axis=0, tiled=True)


def sum_second(terms, idx):
    depth = lax.axis_size("ga")
    if depth > 4:
        return lax.psum(sum_all(terms), "ga")
    pieces = sum_split(terms, [terms[0].shape[0]], depth, 2, idx)[0]
    return sum_all([pieces[0]] + [swap(pieces[d], "ga", d) for d in range(1, depth)])


def gather_ga(own):
    depth = lax.axis_size("ga")
    if depth > 4:
        return own
    return jnp.concatenate([own] + [swap(own, "ga", d) for d in range(1, depth)], axis=0)


def gather_chips(own):
    parts = lax.axis_size("band")
    groups = [list(range(core, parts, 2)) for core in range(2)]
    copies = jnp.broadcast_to(own, (parts // 2, *own.shape))
    got = lax.all_to_all(copies, "band", 0, 0, axis_index_groups=groups)
    return got.reshape(-1, own.shape[1])


def place_bands(first_ref, parts, flat_ref):
    rows = first_ref.shape[0] // parts
    for band in range(parts):
        at = ((band % 2) * (parts // 2) + band // 2) * rows
        flat_ref[at : at + rows, :] = first_ref[band * rows : (band + 1) * rows, :]


def place_offsets(halves_, chips, cuts, idx_ref, flat_ref):
    rows = halves_[0].shape[0] // (chips * cuts)
    for c, ref in enumerate(halves_):
        core = jnp.bitwise_xor(jnp.bitwise_and(idx_ref[0], 1), c)
        for chip in range(chips):
            for z in range(cuts):
                at = (core * chips + chip) * cuts
                at = at + (jnp.bitwise_xor(idx_ref[2], z) if cuts > 1 else 0)
                start = (chip * cuts + z) * rows
                flat_ref[pl.ds(pl.multiple_of(at * rows, 8), rows), :] = ref[start : start + rows, :]


def eliminate(x_ref, vl_ref, vr_ref, r_ref, row_ref, col_ref, base, lo, order, pending):
    hi = lo + BLOCK
    wide = 2 * BLOCK
    rest = order - hi
    row = slice(lo - base, hi - base)
    w = jnp.concatenate(
        leaf(
            [x_ref[lo - base + s : lo - base + s + STRIP, lo:hi] for s in range(0, BLOCK, STRIP)],
            row_ref,
            col_ref,
            pending,
        ),
        axis=0,
    )
    while pending:
        pending.pop(0)()
    if rest:
        v = mm(left3(x_ref[hi - base :, lo:hi]), right3t(w), NT)
        vl_ref[:rest, :] = left3(v)
        vr_ref[:rest, :] = right3t(v)
        near = slice(hi - base, hi - base + BLOCK)
        t = mm(vl_ref[:BLOCK, :], vr_ref[:BLOCK, :], NT)
        x_ref[near, hi : hi + BLOCK] = x_ref[near, hi : hi + BLOCK] - t
    r_ref[:, lo:hi] = right3(w)
    x_ref[row, lo:hi] = w
    if rest:
        x_ref[row, hi:] = jnp.zeros((BLOCK, rest), jnp.float32)

    def update_sums(c, d):
        top = max(c, hi + BLOCK)
        t = mm(vl_ref[top - hi : rest, :], vr_ref[c - hi : d - hi, :], NT)
        x_ref[top - base :, c:d] = x_ref[top - base :, c:d] - t

    def finish_row(c, d):
        t = mm(left3(w), right3(x_ref[row, c:d]))
        x_ref[row, c:d] = t
        r_ref[:, c:d] = right3(t)

    def update_rows(c, d):
        t = mm(vl_ref[:rest, :], r_ref[:, c:d])
        if d <= lo:
            x_ref[hi - base :, c:d] = x_ref[hi - base :, c:d] - t
        else:
            if c < lo:
                x_ref[hi - base :, c:lo] = x_ref[hi - base :, c:lo] - t[:, : lo - c]
            x_ref[hi - base :, lo:hi] = -t[:, lo - c :]

    if rest:
        for c in range(hi, order, wide):
            if max(c, hi + BLOCK) < order:
                pending.append(functools.partial(update_sums, c, min(c + wide, order)))
    for c in range(0, lo, wide):
        pending.append(functools.partial(finish_row, c, min(c + wide, lo)))
    if rest:
        for c in range(0, hi, wide):
            pending.append(functools.partial(update_rows, c, min(c + wide, hi)))


def eliminate_all(x_ref, work, base, first, last, order):
    pending = []
    for lo in range(first, last, BLOCK):
        eliminate(x_ref, *work, base, lo, order, pending)
    for job in pending:
        job()


def head_kernel(parts, head, idx_ref, first_ref, done_ref, rest_ref, mark_ref, x_ref, flat_ref, *work):
    place_bands(first_ref, parts, flat_ref)
    for n, (i, j) in enumerate(lower_blocks(0, head)):
        x_ref[i * BLOCK : (i + 1) * BLOCK, j * BLOCK : (j + 1) * BLOCK] = flat_ref[
            n * BLOCK : (n + 1) * BLOCK, :
        ]
    order = head * BLOCK
    half = order // 2
    eliminate_all(x_ref, work, 0, 0, half, order)
    done_ref[...] = x_ref[:half, :half]
    rest_ref[...] = x_ref[half:, :]
    mark_ref[...] = x_ref[:STRIP, :BLOCK]


def neck_kernel(idx_ref, in_ref, before_ref, x_ref, mark_ref, *work):
    x_ref[...] = in_ref[...]
    half, order = x_ref.shape
    eliminate_all(x_ref, work, half, half, order, order)
    mark_ref[...] = x_ref[:STRIP, :BLOCK]


def tail_kernel(chips, cuts, head, idx_ref, a_ref, b_ref, before_ref, near_ref, far_ref, high_ref, low_ref, *refs):
    parts = 2 * chips
    outs, (x_ref, out_ref, flat_ref), work = refs[:parts], refs[parts : parts + 3], refs[parts + 3 :]
    order = high_ref.shape[0]
    base = head * BLOCK
    place_offsets([near_ref, far_ref], chips, cuts, idx_ref, flat_ref)
    for n, (i, j) in enumerate(lower_blocks(head, order // BLOCK)):
        x_ref[i * BLOCK - base : (i + 1) * BLOCK - base, j * BLOCK : (j + 1) * BLOCK] = flat_ref[
            n * BLOCK : (n + 1) * BLOCK, :
        ]
    half = a_ref.shape[0]
    a, b = halves(a_ref[...]), halves(b_ref[...])
    b_left, b_right = [x[:, :half] for x in b], [x[:, half:] for x in b]
    s_high, s_low = halves(x_ref[:, :base])
    v = mm3(s_high[:, :half], s_low[:, :half], *a, NT)
    v_left = halves(v)
    v = mm3(s_high, s_low, *b, NT)
    v_right = halves(v)
    x_ref[:, :half] = -(mm3(*v_left, *a) + mm3(*v_right, *b_left))
    x_ref[:, half:base] = -mm3(*v_right, *b_right)
    x_ref[:, base:] = x_ref[:, base:] - (mm3(*v_left, *v_left, NT) + mm3(*v_right, *v_right, NT))

    def product(ref, row, first, last):
        x = halves(ref[row : row + last - first, :last])
        out_ref[first:last, :] = mm3(*x, high_ref[:last, :], low_ref[:last, :])

    pending = [
        functools.partial(product, a_ref, 0, 0, half),
        functools.partial(product, b_ref, 0, half, base),
    ]
    for lo in range(base, order, BLOCK):
        eliminate(x_ref, *work, base, lo, order, pending)
        pending.append(functools.partial(product, x_ref, lo - base, lo, lo + BLOCK))
    for job in pending:
        job()
    rows = order // parts
    for d in range(parts):
        at = pl.ds(pl.multiple_of(jnp.bitwise_xor(idx_ref[0], d) * rows, rows), rows)
        outs[d][...] = out_ref[at, :]


def factor_scratch(blocks, rows, order):
    return [
        pltpu.VMEM((len(blocks) * BLOCK, BLOCK), jnp.float32),
        pltpu.VMEM((rows - BLOCK, 3 * BLOCK), jnp.bfloat16),
        pltpu.VMEM((rows - BLOCK, 3 * BLOCK), jnp.bfloat16),
        pltpu.VMEM((3 * BLOCK, order), jnp.bfloat16),
        pltpu.VMEM((BLOCK, BLOCK), jnp.float32),
        pltpu.VMEM((BLOCK * STRIP, BLOCK), jnp.float32),
    ]


def head_factor(first, parts, idx, head):
    rows = head * BLOCK
    half = rows // 2
    return vmem_call(
        functools.partial(head_kernel, parts, head),
        [f32(half, half), f32(half, rows), f32(STRIP, BLOCK)],
        [pltpu.VMEM((rows, rows), jnp.float32)] + factor_scratch(lower_blocks(0, head), rows, rows),
        idx,
        [first],
        cost=3,
    )


def neck_factor(rest, mark, idx):
    half, rows = rest.shape
    return vmem_call(
        neck_kernel,
        [f32(half, rows), f32(STRIP, BLOCK)],
        factor_scratch([], half, rows)[1:],
        idx,
        [rest, mark],
        cost=3,
    )


def tail_product(top, below, mark, second, high, low, chips, cuts, idx, head):
    order, width = high.shape
    rows = order - head * BLOCK
    parts = 2 * chips
    return vmem_call(
        functools.partial(tail_kernel, chips, cuts, head),
        [f32(order // parts, width)] * parts,
        [pltpu.VMEM((rows, order), jnp.float32), pltpu.VMEM((order, width), jnp.float32)]
        + factor_scratch(lower_blocks(head, order // BLOCK), rows, order),
        idx,
        [top, below, mark, *second, high, low],
        cost=25,
        vmem=24,
    )


def local(coeffs):
    band_rows, width = coeffs.shape
    parts = lax.axis_size("band")
    order = band_rows * parts
    columns_all = width * lax.axis_size("ga")
    head = order // BLOCK // 2
    band = lax.axis_index("band")
    idx = jnp.stack([band, band // 2, lax.axis_index("ga")]).astype(jnp.int32)
    pieces = cut_columns(coeffs, band, parts)
    pieces = [pieces[0]] + [swap(pieces[d], "band", d) for d in range(1, parts)]
    keep, send, high, low = gram(pieces, idx, columns_all, head)
    first, second = [sum_chips(p) for p in sum_band(keep, send, head, order, idx)]
    first = sum_first(first)
    second, first = lax.optimization_barrier((sum_second(second, idx), first))
    second = gather_ga(second)
    top, rest, mark = head_factor(first, parts, idx, head)
    second, mark = lax.optimization_barrier((second, mark))
    second = gather_chips(second)
    below, mark = neck_factor(rest, mark, idx)
    second, mark = lax.optimization_barrier((second, mark))
    cuts = lax.axis_size("ga") if lax.axis_size("ga") <= 4 else 1
    result = tail_product(
        top, below, mark, (second, swap(second, "band", 1)), high, low, parts // 2, cuts, idx, head
    )
    result = [result[0]] + [swap(result[d], "band", d) for d in range(1, parts)]
    return join_columns(result, idx)


def solution(mesh):
    return jax.shard_map(
        local,
        mesh=mesh,
        in_specs=(P("band", "ga"),),
        out_specs=P("band", "ga"),
        check_vma=False,
    )
```

time: 156 us -> 153 us (0.981)
  Pallas kernels: 43.2 us -> 38.5 us
  local copies, waits for them, and re-layouts: 3.3 us -> 6.4 us
    pallas_call x10 -> x7, Pallas kernels: 43.2 us -> 38.5 us  [vmem_call(): pl.pallas_call(kernel, out_shape=shapes, in_specs=[pl.BlockSpec(memory_sp...]
    all_to_all x1, waiting for transfers between devices: 4.33 us -> 2.5 us  [gather_chips(): got = lax.all_to_all(copies, 'band', 0, 0, axis_index_groups=groups)]
    dynamic_slice x0 -> x1, local copies, waits for them, and re-layouts: none -> 1.76 us  [cut_columns(): lax.dynamic_slice_in_dim(x, (band ^ d) * width, width, 1)]
    unnamed x34 -> x12, local copies, waits for them, and re-layouts: 2.35 us -> 3.68 us
    ppermute x32 -> x31, waiting for transfers between devices: 55.6 us -> 56.4 us  [swap(): lax.ppermute(x, axis, [(i, i ^ d) for i in range(lax.axis_size(axis))])]
    ppermute x32 -> x31, starting transfers between devices: 35.9 us -> 35.5 us  [swap(): lax.ppermute(x, axis, [(i, i ^ d) for i in range(lax.axis_size(axis))])]
  transfers between devices with their start and end apart: 33 -> 32, of which waited for: 15 -> 18; matrix products, arithmetic and copies ran while one was open for 0% -> 0% of each run, Pallas kernels for 10% -> 9%
where the time goes in v1:
time: 153 us
  waiting for transfers between devices  58.9 us (38%)
  starting transfers between devices  39.2 us (26%)
  Pallas kernels  38.5 us (25%)
  blocking collectives  9.86 us (6%)
  local copies, waits for them, and re-layouts  6.4 us (4%)
    ppermute x31, waiting for transfers between devices, swap(): lax.ppermute(x, axis, [(i, i ^ d) for i in range(lax.axis_size(axis))])  56.4 us
    pallas_call x7, Pallas kernels, vmem_call(): pl.pallas_call(kernel, out_shape=shapes, in_specs=[pl.BlockSpec(memory_sp...  38.5 us
    ppermute x31, starting transfers between devices, swap(): lax.ppermute(x, axis, [(i, i ^ d) for i in range(lax.axis_size(axis))])  35.5 us
    all_gather x1, blocking collectives, sum_first(): return lax.all_gather(total, 'band', axis=0, tiled=True)  9.86 us
    all_to_all x1, starting transfers between devices, gather_chips(): got = lax.all_to_all(copies, 'band', 0, 0, axis_index_groups=groups)  3.68 us
    unnamed x12, local copies, waits for them, and re-layouts  3.68 us
  transfers between devices with their start and end apart: 32, of which 18 were waited for; matrix products, arithmetic and copies ran while one was open for 0% of the time, Pallas kernels for 9%

profile of v1, /device:TPU:0, one launch (start us, length us, event | category | flops | bytes accessed | tf_op | source)
XLA Modules:
  0.0 153.2 jit_solution(15788400210489299690)
XLA Ops:
  0.0 1.8 %constant_dynamic-slice_fusion = (f32[128,512]{1,0:T(8,128)S(1)}, f32[128,512]{1,0:T(8,128)S(1)}, f32[128,512]{1,0:T(8,128)S(1)}, f32[128,512]{1,0:T(8,128)S(1)}...) fusion(f32[128,4096]{1,0:T(8,128)} %param.1, ...), kind=kLoop, calls=%fused_computation.4 | loop fusion | bytes 4194336 | tf_op jit(solution)/shard_map/dynamic_slice | solution.py:145
  1.8 3.4 %collective-permute-start.6 = (f32[128,512]{1,0:T(8,128)S(1)}, f32[128,512]{1,0:T(8,128)S(1)}, u32[]{:S(2)}, u32[]{:S(2)}) collective-permute-start(f32[128,512]{1,0:T(8,128)S(1)} %get-tuple-element.75), channel_id=1, source_target_pairs={{0,28},{4,24},{8,20},{12,16},{16,12},{20,8},{24,4},{28,0},{1,29},{... | collective-permute-start | bytes 786440 | tf_op jit(solution)/shard_map/ppermute | solution.py:245
  6.0 1.5 collective-permute-start.3
  8.7 3.2 %collective-permute-done.6.refs_7_ = f32[128,512]{1,0:T(8,128)S(1)} collective-permute-done((f32[128,512]{1,0:T(8,128)S(1)}, f32[128,512]{1,0:T(8,128)S(1)}, u32[]{:S(2)}, u32[]{:S(2)}) %collective-permute-start.6) | collective-permute-done | bytes 262176 | tf_op jit(solution)/shard_map/ppermute | solution.py:245
  12.7 4.8 %collective-permute-done.4.refs_5_ = f32[128,512]{1,0:T(8,128)S(1)} collective-permute-done((f32[128,512]{1,0:T(8,128)S(1)}, f32[128,512]{1,0:T(8,128)S(1)}, u32[]{:S(2)}, u32[]{:S(2)}) %collective-permute-start.4) | collective-permute-done | bytes 262176 | tf_op jit(solution)/shard_map/ppermute | solution.py:245
  17.6 2.4 %collective-permute-start.5 = (f32[128,512]{1,0:T(8,128)S(1)}, f32[128,512]{1,0:T(8,128)S(1)}, u32[]{:S(2)}, u32[]{:S(2)}) collective-permute-start(f32[128,512]{1,0:T(8,128)S(1)} %get-tuple-element.82), channel_id=1, source_target_pairs={{0,24},{4,28},{8,16},{12,20},{16,8},{20,12},{24,0},{28,4},{1,25},{... | collective-permute-start | bytes 786440 | tf_op jit(solution)/shard_map/ppermute | solution.py:245
  20.1 4.0 %collective-permute-done.3.refs_4_ = f32[128,512]{1,0:T(8,128)S(1)} collective-permute-done((f32[128,512]{1,0:T(8,128)S(1)}, f32[128,512]{1,0:T(8,128)S(1)}, u32[]{:S(2)}, u32[]{:S(2)}) %collective-permute-start.3) | collective-permute-done | bytes 262176 | tf_op jit(solution)/shard_map/ppermute | solution.py:245
  24.1 4.8 %collective-permute-done.5.refs_6_ = f32[128,512]{1,0:T(8,128)S(1)} collective-permute-done((f32[128,512]{1,0:T(8,128)S(1)}, f32[128,512]{1,0:T(8,128)S(1)}, u32[]{:S(2)}, u32[]{:S(2)}) %collective-permute-start.5) | collective-permute-done | bytes 262176 | tf_op jit(solution)/shard_map/ppermute | solution.py:245
  28.9 3.5 %shard_map.17 = (f32[2304,128]{1,0:T(8,128)S(1)}, f32[2304,128]{1,0:T(8,128)S(1)}, bf16[1024,512]{1,0:T(8,128)(2,1)S(1)}, bf16[1024,512]{1,0:T(8,128)(2,1)S(1)}) custom-call(s32[3]{0:T(128)S(1)} %pad_add_fusion.idx_ref, f32[128,512]{1,0:T(8,128)S(1)} %get-tuple-element.81.refs_0_, f32[128,512]{1,0:T(8,128)S(1)} %collective-permute-done.refs_1_, ...), custom_call_target="tpu_custom_call" | custom-call | flops 1000000000 | tf_op jit(solution)/shard_map/pallas_call | solution.py:126
  32.5 2.8 %collective-permute-done.7.refs_1_ = f32[2304,128]{1,0:T(8,128)S(1)} collective-permute-done((f32[2304,128]{1,0:T(8,128)S(1)}, f32[2304,128]{1,0:T(8,128)S(1)}, u32[]{:S(2)}, u32[]{:S(2)}) %collective-permute-start.7) | collective-permute-done | bytes 1179680 | tf_op jit(solution)/shard_map/ppermute | solution.py:245
  36.1 2.3 %collective-permute-start.14 = (f32[160,128]{1,0:T(8,128)S(1)}, f32[160,128]{1,0:T(8,128)S(1)}, u32[]{:S(2)}, u32[]{:S(2)}) collective-permute-start(f32[160,128]{1,0:T(8,128)S(1)} %get-tuple-element.51), channel_id=1, source_target_pairs={{0,8},{4,12},{8,0},{12,4},{16,24},{20,28},{24,16},{28,20},{1,9},{5... | collective-permute-start | bytes 245768 | tf_op jit(solution)/shard_map/ppermute | solution.py:245
  38.4 1.5 collective-permute-start.15
  41.1 2.5 %collective-permute-done.15 = f32[160,128]{1,0:T(8,128)S(1)} collective-permute-done((f32[160,128]{1,0:T(8,128)S(1)}, f32[160,128]{1,0:T(8,128)S(1)}, u32[]{:S(2)}, u32[]{:S(2)}) %collective-permute-start.15) | collective-permute-done | bytes 81952 | tf_op jit(solution)/shard_map/ppermute | solution.py:245
  43.7 1.6 %collective-permute-done.16 = f32[160,128]{1,0:T(8,128)S(1)} collective-permute-done((f32[160,128]{1,0:T(8,128)S(1)}, f32[160,128]{1,0:T(8,128)S(1)}, u32[]{:S(2)}, u32[]{:S(2)}) %collective-permute-start.16) | collective-permute-done | bytes 81952 | tf_op jit(solution)/shard_map/ppermute | solution.py:245
  45.3 3.7 %collective-permute-start.19 = (f32[160,128]{1,0:T(8,128)S(1)}, f32[160,128]{1,0:T(8,128)S(1)}, u32[]{:S(2)}, u32[]{:S(2)}) collective-permute-start(f32[160,128]{1,0:T(8,128)S(1)} %add_add_fusion.1), channel_id=1, source_target_pairs={{0,3},{1,2},{2,1},{3,0},{4,7},{5,6},{6,5},{7,4},{8,11},{9,10},{10,... | collective-permute-start | bytes 245768 | tf_op jit(solution)/shard_map/ppermute | solution.py:245
  51.6 1.6 %collective-permute-start.10 = (f32[416,128]{1,0:T(8,128)S(1)}, f32[416,128]{1,0:T(8,128)S(1)}, u32[]{:S(2)}, u32[]{:S(2)}) collective-permute-start(f32[416,128]{1,0:T(8,128)S(1)} %get-tuple-element.45), channel_id=1, source_target_pairs={{0,24},{4,28},{8,16},{12,20},{16,8},{20,12},{24,0},{28,4},{1,25},{... | collective-permute-start | bytes 638984 | tf_op jit(solution)/shard_map/ppermute | solution.py:245
  53.2 1.6 %collective-permute-done.18 = f32[160,128]{1,0:T(8,128)S(1)} collective-permute-done((f32[160,128]{1,0:T(8,128)S(1)}, f32[160,128]{1,0:T(8,128)S(1)}, u32[]{:S(2)}, u32[]{:S(2)}) %collective-permute-start.18) | collective-permute-done | bytes 81952 | tf_op jit(solution)/shard_map/ppermute | solution.py:245
  54.9 2.0 %collective-permute-done.8.refs_1_ = f32[416,128]{1,0:T(8,128)S(1)} collective-permute-done((f32[416,128]{1,0:T(8,128)S(1)}, f32[416,128]{1,0:T(8,128)S(1)}, u32[]{:S(2)}, u32[]{:S(2)}) %collective-permute-start.8) | collective-permute-done | bytes 213024 | tf_op jit(solution)/shard_map/ppermute | solution.py:245
  56.9 2.9 %collective-permute-done.9.refs_2_ = f32[416,128]{1,0:T(8,128)S(1)} collective-permute-done((f32[416,128]{1,0:T(8,128)S(1)}, f32[416,128]{1,0:T(8,128)S(1)}, u32[]{:S(2)}, u32[]{:S(2)}) %collective-permute-start.9) | collective-permute-done | bytes 213024 | tf_op jit(solution)/shard_map/ppermute | solution.py:245
  61.8 2.6 %collective-permute-start.12 = (f32[104,128]{1,0:T(8,128)S(1)}, f32[104,128]{1,0:T(8,128)S(1)}, u32[]{:S(2)}, u32[]{:S(2)}) collective-permute-start(f32[104,128]{1,0:T(8,128)S(1)} %get-tuple-element.48), channel_id=1, source_target_pairs={{0,2},{1,3},{2,0},{3,1},{4,6},{5,7},{6,4},{7,5},{8,10},{9,11},{10,... | collective-permute-start | bytes 159752 | tf_op jit(solution)/shard_map/ppermute | solution.py:245
  64.8 9.9 %all_gather.3.first_ref = f32[1280,128]{1,0:T(8,128)S(1)} all-gather(f32[160,128]{1,0:T(8,128)S(1)} %add_add_fusion), channel_id=1, replica_groups=mesh['band'=8,'ga'=4] {'band'}, dimensions={0}, use_global_device_ids=true | all-gather | bytes 737280 | tf_op jit(solution)/shard_map/all_gather | solution.py:271
  74.7 3.5 %collective-permute-start.22 = (f32[104,128]{1,0:T(8,128)S(1)}, f32[104,128]{1,0:T(8,128)S(1)}, u32[]{:S(2)}, u32[]{:S(2)}) collective-permute-start(f32[104,128]{1,0:T(8,128)S(1)} %add_add_fusion.2), channel_id=1, source_target_pairs={{0,3},{1,2},{2,1},{3,0},{4,7},{5,6},{6,5},{7,4},{8,11},{9,10},{10,... | collective-permute-start | bytes 159752 | tf_op jit(solution)/shard_map/ppermute | solution.py:245
  79.2 7.4 %shard_map.20 = (f32[256,256]{1,0:T(8,128)S(1)}, f32[256,512]{1,0:T(8,128)S(1)}, f32[8,128]{1,0:T(8,128)S(1)}) custom-call(s32[3]{0:T(128)S(1)} %pad_add_fusion.idx_ref, f32[1280,128]{1,0:T(8,128)S(1)} %all_gather.3.first_ref), custom_call_target="tpu_custom_call" | custom-call | flops 3000000000 | tf_op jit(solution)/shard_map/pallas_call | solution.py:126
  88.4 3.7 %all-to-all-start = ((f32[4,416,128]{2,1,0:T(8,128)}), f32[4,416,128]{2,1,0:T(8,128)S(1)}, u32[]{:S(2)}, u32[]{:S(2)}) async-start(f32[4,416,128]{2,1,0:T(8,128)} %broadcast_in_dim.3), calls=%async_computation | async-start | bytes 1703936 | tf_op jit(solution)/shard_map/all_to_all | solution.py:293
  93.1 6.9 %shard_map.21 = (f32[256,512]{1,0:T(8,128)S(1)}, f32[8,128]{1,0:T(8,128)S(1)}) custom-call(s32[3]{0:T(128)S(1)} %pad_add_fusion.idx_ref, f32[256,512]{1,0:T(8,128)S(1)} %copy-done.3, f32[8,128]{1,0:T(8,128)S(1)} %get-tuple-element.59.before_ref), custom_call_target="tpu_custom_call" | custom-call | flops 3000000000 | tf_op jit(solution)/shard_map/pallas_call | solution.py:126
  100.9 2.5 %all-to-all-done = f32[4,416,128]{2,1,0:T(8,128)S(1)} async-done(((f32[4,416,128]{2,1,0:T(8,128)}), f32[4,416,128]{2,1,0:T(8,128)S(1)}, u32[]{:S(2)}, u32[]{:S(2)}) %all-to-all-start) | async-done | bytes 852000 | tf_op jit(solution)/shard_map/all_to_all | solution.py:293
  103.4 2.4 %collective-permute-done.23.far_ref = f32[1664,128]{1,0:T(8,128)S(1)} collective-permute-done((f32[1664,128]{1,0:T(8,128)S(1)}, f32[1664,128]{1,0:T(8,128)S(1)}, u32[]{:S(2)}, u32[]{:S(2)}) %collective-permute-start.23) | collective-permute-done | bytes 852000 | tf_op jit(solution)/shard_map/ppermute | solution.py:245
  106.8 17.4 %shard_map.22 = (f32[128,512]{1,0:T(8,128)S(1)}, f32[128,512]{1,0:T(8,128)S(1)}, f32[128,512]{1,0:T(8,128)S(1)}, f32[128,512]{1,0:T(8,128)S(1)}, f32[128,512]{1,...) custom-call(s32[3]{0:T(128)S(1)} %pad_add_fusion.idx_ref, ...), custom_call_target="tpu_custom_call" | custom-call | flops 24999999488 | tf_op jit(solution)/shard_map/pallas_call | solution.py:126
  129.3 4.2 %collective-permute-done.25.refs_2_ = f32[128,512]{1,0:T(8,128)S(1)} collective-permute-done((f32[128,512]{1,0:T(8,128)S(1)}, f32[128,512]{1,0:T(8,128)S(1)}, u32[]{:S(2)}, u32[]{:S(2)}) %collective-permute-start.25) | collective-permute-done | bytes 262176 | tf_op jit(solution)/shard_map/ppermute | solution.py:245
  133.5 4.5 %collective-permute-done.26.refs_3_ = f32[128,512]{1,0:T(8,128)S(1)} collective-permute-done((f32[128,512]{1,0:T(8,128)S(1)}, f32[128,512]{1,0:T(8,128)S(1)}, u32[]{:S(2)}, u32[]{:S(2)}) %collective-permute-start.26) | collective-permute-done | bytes 262176 | tf_op jit(solution)/shard_map/ppermute | solution.py:245
  138.1 13.1 %collective-permute-done.28.refs_5_ = f32[128,512]{1,0:T(8,128)S(1)} collective-permute-done((f32[128,512]{1,0:T(8,128)S(1)}, f32[128,512]{1,0:T(8,128)S(1)}, u32[]{:S(2)}, u32[]{:S(2)}) %collective-permute-start.28) | collective-permute-done | bytes 262176 | tf_op jit(solution)/shard_map/ppermute | solution.py:245
  151.2 2.0 %shard_map.23 = f32[128,4096]{1,0:T(8,128)} custom-call(s32[3]{0:T(128)S(1)} %pad_add_fusion.idx_ref, f32[128,512]{1,0:T(8,128)S(1)} %get-tuple-element.67.refs_0_, f32[128,512]{1,0:T(8,128)S(1)} %collective-permute-done.24.refs_1_, f32[128,512]{1,0:T(8,128)S(1)} %collective-permute-done.25.refs_2_, f32[128,512]{1,0:T(8,128)S(1)} %collective-permute-done.26.refs_3_, ...), custom_call_target="tpu_custom_call" | custom-call | flops 1000000000 | tf_op jit(solution)/shard_map/pallas_call | solution.py:126
  (59 shorter events, 20.9 us)
Async XLA Ops:
  1.8 10.1 %collective-permute-start.6 = (f32[128,512]{1,0:T(8,128)S(1)}, f32[128,512]{1,0:T(8,128)S(1)}, u32[]{:S(2)}, u32[]{:S(2)}) collective-permute-start(f32[128,512]{1,0:T(8,128)S(1)} %get-tuple-element.75), channel_id=1, source_target_pairs={{0,28},{4,24},{8,20},{12,16},{16,12},{20,8},{24,4},{28,0},{1,29},{... | collective-permute-start | bytes 786440 | tf_op jit(solution)/shard_map/ppermute | solution.py:245
  5.2 12.4 %collective-permute-start.4 = (f32[128,512]{1,0:T(8,128)S(1)}, f32[128,512]{1,0:T(8,128)S(1)}, u32[]{:S(2)}, u32[]{:S(2)}) collective-permute-start(f32[128,512]{1,0:T(8,128)S(1)} %get-tuple-element.76), channel_id=1, source_target_pairs={{0,20},{4,16},{8,28},{12,24},{16,4},{20,0},{24,12},{28,8},{1,21},{... | collective-permute-start | bytes 786440 | tf_op jit(solution)/shard_map/ppermute | solution.py:245
  6.0 18.1 %collective-permute-start.3 = (f32[128,512]{1,0:T(8,128)S(1)}, f32[128,512]{1,0:T(8,128)S(1)}, u32[]{:S(2)}, u32[]{:S(2)}) collective-permute-start(f32[128,512]{1,0:T(8,128)S(1)} %get-tuple-element.77), channel_id=1, source_target_pairs={{0,16},{4,20},{8,24},{12,28},{16,0},{20,4},{24,8},{28,12},{1,17},{... | collective-permute-start | bytes 786440 | tf_op jit(solution)/shard_map/ppermute | solution.py:245
  7.5 16.6 %collective-permute-start.2 = (f32[128,512]{1,0:T(8,128)S(1)}, f32[128,512]{1,0:T(8,128)S(1)}, u32[]{:S(2)}, u32[]{:S(2)}) collective-permute-start(f32[128,512]{1,0:T(8,128)S(1)} %get-tuple-element.78), channel_id=1, source_target_pairs={{0,12},{4,8},{8,4},{12,0},{16,28},{20,24},{24,20},{28,16},{1,13},{... | collective-permute-start | bytes 786440 | tf_op jit(solution)/shard_map/ppermute | solution.py:245
  7.5 16.7 %collective-permute-start.1 = (f32[128,512]{1,0:T(8,128)S(1)}, f32[128,512]{1,0:T(8,128)S(1)}, u32[]{:S(2)}, u32[]{:S(2)}) collective-permute-start(f32[128,512]{1,0:T(8,128)S(1)} %get-tuple-element.79), channel_id=1, source_target_pairs={{0,8},{4,12},{8,0},{12,4},{16,24},{20,28},{24,16},{28,20},{1,9},{5... | collective-permute-start | bytes 786440 | tf_op jit(solution)/shard_map/ppermute | solution.py:245
  11.9 12.2 %collective-permute-start = (f32[128,512]{1,0:T(8,128)S(1)}, f32[128,512]{1,0:T(8,128)S(1)}, u32[]{:S(2)}, u32[]{:S(2)}) collective-permute-start(f32[128,512]{1,0:T(8,128)S(1)} %get-tuple-element.80), channel_id=1, source_target_pairs={{0,4},{4,0},{8,12},{12,8},{16,20},{20,16},{24,28},{28,24},{1,5},{5... | collective-permute-start | bytes 786440 | tf_op jit(solution)/shard_map/ppermute | solution.py:245
  17.6 11.4 %collective-permute-start.5 = (f32[128,512]{1,0:T(8,128)S(1)}, f32[128,512]{1,0:T(8,128)S(1)}, u32[]{:S(2)}, u32[]{:S(2)}) collective-permute-start(f32[128,512]{1,0:T(8,128)S(1)} %get-tuple-element.82), channel_id=1, source_target_pairs={{0,24},{4,28},{8,16},{12,20},{16,8},{20,12},{24,0},{28,4},{1,25},{... | collective-permute-start | bytes 786440 | tf_op jit(solution)/shard_map/ppermute | solution.py:245
  32.4 2.9 %collective-permute-start.7 = (f32[2304,128]{1,0:T(8,128)S(1)}, f32[2304,128]{1,0:T(8,128)S(1)}, u32[]{:S(2)}, u32[]{:S(2)}) collective-permute-start(f32[2304,128]{1,0:T(8,128)S(1)} %get-tuple-element.41), channel_id=1, source_target_pairs={{0,4},{4,0},{8,12},{12,8},{16,20},{20,16},{24,28},{28,24},{1,5},{5... | collective-permute-start | bytes 3538952 | tf_op jit(solution)/shard_map/ppermute | solution.py:245
  36.1 5.1 %collective-permute-start.14 = (f32[160,128]{1,0:T(8,128)S(1)}, f32[160,128]{1,0:T(8,128)S(1)}, u32[]{:S(2)}, u32[]{:S(2)}) collective-permute-start(f32[160,128]{1,0:T(8,128)S(1)} %get-tuple-element.51), channel_id=1, source_target_pairs={{0,8},{4,12},{8,0},{12,4},{16,24},{20,28},{24,16},{28,20},{1,9},{5... | collective-permute-start | bytes 245768 | tf_op jit(solution)/shard_map/ppermute | solution.py:245
  38.4 5.3 %collective-permute-start.15 = (f32[160,128]{1,0:T(8,128)S(1)}, f32[160,128]{1,0:T(8,128)S(1)}, u32[]{:S(2)}, u32[]{:S(2)}) collective-permute-start(f32[160,128]{1,0:T(8,128)S(1)} %get-tuple-element.52), channel_id=1, source_target_pairs={{0,16},{4,20},{8,24},{12,28},{16,0},{20,4},{24,8},{28,12},{1,17},{... | collective-permute-start | bytes 245768 | tf_op jit(solution)/shard_map/ppermute | solution.py:245
  39.9 5.3 %collective-permute-start.16 = (f32[160,128]{1,0:T(8,128)S(1)}, f32[160,128]{1,0:T(8,128)S(1)}, u32[]{:S(2)}, u32[]{:S(2)}) collective-permute-start(f32[160,128]{1,0:T(8,128)S(1)} %get-tuple-element.53), channel_id=1, source_target_pairs={{0,24},{4,28},{8,16},{12,20},{16,8},{20,12},{24,0},{28,4},{1,25},{... | collective-permute-start | bytes 245768 | tf_op jit(solution)/shard_map/ppermute | solution.py:245
  45.3 6.3 %collective-permute-start.19 = (f32[160,128]{1,0:T(8,128)S(1)}, f32[160,128]{1,0:T(8,128)S(1)}, u32[]{:S(2)}, u32[]{:S(2)}) collective-permute-start(f32[160,128]{1,0:T(8,128)S(1)} %add_add_fusion.1), channel_id=1, source_target_pairs={{0,3},{1,2},{2,1},{3,0},{4,7},{5,6},{6,5},{7,4},{8,11},{9,10},{10,... | collective-permute-start | bytes 245768 | tf_op jit(solution)/shard_map/ppermute | solution.py:245
  48.9 5.9 %collective-permute-start.18 = (f32[160,128]{1,0:T(8,128)S(1)}, f32[160,128]{1,0:T(8,128)S(1)}, u32[]{:S(2)}, u32[]{:S(2)}) collective-permute-start(f32[160,128]{1,0:T(8,128)S(1)} %add_add_fusion.1), channel_id=1, source_target_pairs={{0,2},{1,3},{2,0},{3,1},{4,6},{5,7},{6,4},{7,5},{8,10},{9,11},{10,... | collective-permute-start | bytes 245768 | tf_op jit(solution)/shard_map/ppermute | solution.py:245
  48.9 5.9 %collective-permute-start.17 = (f32[160,128]{1,0:T(8,128)S(1)}, f32[160,128]{1,0:T(8,128)S(1)}, u32[]{:S(2)}, u32[]{:S(2)}) collective-permute-start(f32[160,128]{1,0:T(8,128)S(1)} %add_add_fusion.1), channel_id=1, source_target_pairs={{0,1},{1,0},{2,3},{3,2},{4,5},{5,4},{6,7},{7,6},{8,9},{9,8},{10,11... | collective-permute-start | bytes 245768 | tf_op jit(solution)/shard_map/ppermute | solution.py:245
  49.7 7.2 %collective-permute-start.8 = (f32[416,128]{1,0:T(8,128)S(1)}, f32[416,128]{1,0:T(8,128)S(1)}, u32[]{:S(2)}, u32[]{:S(2)}) collective-permute-start(f32[416,128]{1,0:T(8,128)S(1)} %get-tuple-element.43), channel_id=1, source_target_pairs={{0,8},{4,12},{8,0},{12,4},{16,24},{20,28},{24,16},{28,20},{1,9},{5... | collective-permute-start | bytes 638984 | tf_op jit(solution)/shard_map/ppermute | solution.py:245
  50.3 9.5 %collective-permute-start.9 = (f32[416,128]{1,0:T(8,128)S(1)}, f32[416,128]{1,0:T(8,128)S(1)}, u32[]{:S(2)}, u32[]{:S(2)}) collective-permute-start(f32[416,128]{1,0:T(8,128)S(1)} %get-tuple-element.44), channel_id=1, source_target_pairs={{0,16},{4,20},{8,24},{12,28},{16,0},{20,4},{24,8},{28,12},{1,17},{... | collective-permute-start | bytes 638984 | tf_op jit(solution)/shard_map/ppermute | solution.py:245
  51.6 8.2 %collective-permute-start.10 = (f32[416,128]{1,0:T(8,128)S(1)}, f32[416,128]{1,0:T(8,128)S(1)}, u32[]{:S(2)}, u32[]{:S(2)}) collective-permute-start(f32[416,128]{1,0:T(8,128)S(1)} %get-tuple-element.45), channel_id=1, source_target_pairs={{0,24},{4,28},{8,16},{12,20},{16,8},{20,12},{24,0},{28,4},{1,25},{... | collective-permute-start | bytes 638984 | tf_op jit(solution)/shard_map/ppermute | solution.py:245
  60.3 14.3 %collective-permute-start.11 = (f32[104,128]{1,0:T(8,128)S(1)}, f32[104,128]{1,0:T(8,128)S(1)}, u32[]{:S(2)}, u32[]{:S(2)}) collective-permute-start(f32[104,128]{1,0:T(8,128)S(1)} %get-tuple-element.47), channel_id=1, source_target_pairs={{0,1},{1,0},{2,3},{3,2},{4,5},{5,4},{6,7},{7,6},{8,9},{9,8},{10,11... | collective-permute-start | bytes 159752 | tf_op jit(solution)/shard_map/ppermute | solution.py:245
  61.8 12.9 %collective-permute-start.12 = (f32[104,128]{1,0:T(8,128)S(1)}, f32[104,128]{1,0:T(8,128)S(1)}, u32[]{:S(2)}, u32[]{:S(2)}) collective-permute-start(f32[104,128]{1,0:T(8,128)S(1)} %get-tuple-element.48), channel_id=1, source_target_pairs={{0,2},{1,3},{2,0},{3,1},{4,6},{5,7},{6,4},{7,5},{8,10},{9,11},{10,... | collective-permute-start | bytes 159752 | tf_op jit(solution)/shard_map/ppermute | solution.py:245
  64.4 10.2 %collective-permute-start.13 = (f32[104,128]{1,0:T(8,128)S(1)}, f32[104,128]{1,0:T(8,128)S(1)}, u32[]{:S(2)}, u32[]{:S(2)}) collective-permute-start(f32[104,128]{1,0:T(8,128)S(1)} %get-tuple-element.49), channel_id=1, source_target_pairs={{0,3},{1,2},{2,1},{3,0},{4,7},{5,6},{6,5},{7,4},{8,11},{9,10},{10,... | collective-permute-start | bytes 159752 | tf_op jit(solution)/shard_map/ppermute | solution.py:245
  74.7 12.7 %collective-permute-start.22 = (f32[104,128]{1,0:T(8,128)S(1)}, f32[104,128]{1,0:T(8,128)S(1)}, u32[]{:S(2)}, u32[]{:S(2)}) collective-permute-start(f32[104,128]{1,0:T(8,128)S(1)} %add_add_fusion.2), channel_id=1, source_target_pairs={{0,3},{1,2},{2,1},{3,0},{4,7},{5,6},{6,5},{7,4},{8,11},{9,10},{10,... | collective-permute-start | bytes 159752 | tf_op jit(solution)/shard_map/ppermute | solution.py:245
  78.2 9.3 %collective-permute-start.21 = (f32[104,128]{1,0:T(8,128)S(1)}, f32[104,128]{1,0:T(8,128)S(1)}, u32[]{:S(2)}, u32[]{:S(2)}) collective-permute-start(f32[104,128]{1,0:T(8,128)S(1)} %add_add_fusion.2), channel_id=1, source_target_pairs={{0,2},{1,3},{2,0},{3,1},{4,6},{5,7},{6,4},{7,5},{8,10},{9,11},{10,... | collective-permute-start | bytes 159752 | tf_op jit(solution)/shard_map/ppermute | solution.py:245
  78.2 9.3 %collective-permute-start.20 = (f32[104,128]{1,0:T(8,128)S(1)}, f32[104,128]{1,0:T(8,128)S(1)}, u32[]{:S(2)}, u32[]{:S(2)}) collective-permute-start(f32[104,128]{1,0:T(8,128)S(1)} %add_add_fusion.2), channel_id=1, source_target_pairs={{0,1},{1,0},{2,3},{3,2},{4,5},{5,4},{6,7},{7,6},{8,9},{9,8},{10,11... | collective-permute-start | bytes 159752 | tf_op jit(solution)/shard_map/ppermute | solution.py:245
  88.4 15.0 %all-to-all-start = ((f32[4,416,128]{2,1,0:T(8,128)}), f32[4,416,128]{2,1,0:T(8,128)S(1)}, u32[]{:S(2)}, u32[]{:S(2)}) async-start(f32[4,416,128]{2,1,0:T(8,128)} %broadcast_in_dim.3), calls=%async_computation | async-start | bytes 1703936 | tf_op jit(solution)/shard_map/all_to_all | solution.py:293
  103.4 2.4 %collective-permute-start.23 = (f32[1664,128]{1,0:T(8,128)S(1)}, f32[1664,128]{1,0:T(8,128)S(1)}, u32[]{:S(2)}, u32[]{:S(2)}) collective-permute-start(f32[1664,128]{1,0:T(8,128)S(1)} %bitcast.4), channel_id=1, source_target_pairs={{0,4},{4,0},{8,12},{12,8},{16,20},{20,16},{24,28},{28,24},{1,5},{5... | collective-permute-start | bytes 2555912 | tf_op jit(solution)/shard_map/ppermute | solution.py:245
  124.2 3.7 %collective-permute-start.24 = (f32[128,512]{1,0:T(8,128)S(1)}, f32[128,512]{1,0:T(8,128)S(1)}, u32[]{:S(2)}, u32[]{:S(2)}) collective-permute-start(f32[128,512]{1,0:T(8,128)S(1)} %get-tuple-element.68), channel_id=1, source_target_pairs={{0,4},{4,0},{8,12},{12,8},{16,20},{20,16},{24,28},{28,24},{1,5},{5... | collective-permute-start | bytes 786440 | tf_op jit(solution)/shard_map/ppermute | solution.py:245
  124.4 9.1 %collective-permute-start.25 = (f32[128,512]{1,0:T(8,128)S(1)}, f32[128,512]{1,0:T(8,128)S(1)}, u32[]{:S(2)}, u32[]{:S(2)}) collective-permute-start(f32[128,512]{1,0:T(8,128)S(1)} %get-tuple-element.69), channel_id=1, source_target_pairs={{0,8},{4,12},{8,0},{12,4},{16,24},{20,28},{24,16},{28,20},{1,9},{5... | collective-permute-start | bytes 786440 | tf_op jit(solution)/shard_map/ppermute | solution.py:245
  125.8 12.3 %collective-permute-start.26 = (f32[128,512]{1,0:T(8,128)S(1)}, f32[128,512]{1,0:T(8,128)S(1)}, u32[]{:S(2)}, u32[]{:S(2)}) collective-permute-start(f32[128,512]{1,0:T(8,128)S(1)} %get-tuple-element.70), channel_id=1, source_target_pairs={{0,12},{4,8},{8,4},{12,0},{16,28},{20,24},{24,20},{28,16},{1,13},{... | collective-permute-start | bytes 786440 | tf_op jit(solution)/shard_map/ppermute | solution.py:245
  126.1 12.0 %collective-permute-start.27 = (f32[128,512]{1,0:T(8,128)S(1)}, f32[128,512]{1,0:T(8,128)S(1)}, u32[]{:S(2)}, u32[]{:S(2)}) collective-permute-start(f32[128,512]{1,0:T(8,128)S(1)} %get-tuple-element.71), channel_id=1, source_target_pairs={{0,16},{4,20},{8,24},{12,28},{16,0},{20,4},{24,8},{28,12},{1,17},{... | collective-permute-start | bytes 786440 | tf_op jit(solution)/shard_map/ppermute | solution.py:245
  127.6 23.6 %collective-permute-start.28 = (f32[128,512]{1,0:T(8,128)S(1)}, f32[128,512]{1,0:T(8,128)S(1)}, u32[]{:S(2)}, u32[]{:S(2)}) collective-permute-start(f32[128,512]{1,0:T(8,128)S(1)} %get-tuple-element.72), channel_id=1, source_target_pairs={{0,20},{4,16},{8,28},{12,24},{16,4},{20,0},{24,12},{28,8},{1,21},{... | collective-permute-start | bytes 786440 | tf_op jit(solution)/shard_map/ppermute | solution.py:245
  127.9 23.3 %collective-permute-start.29 = (f32[128,512]{1,0:T(8,128)S(1)}, f32[128,512]{1,0:T(8,128)S(1)}, u32[]{:S(2)}, u32[]{:S(2)}) collective-permute-start(f32[128,512]{1,0:T(8,128)S(1)} %get-tuple-element.73), channel_id=1, source_target_pairs={{0,24},{4,28},{8,16},{12,20},{16,8},{20,12},{24,0},{28,4},{1,25},{... | collective-permute-start | bytes 786440 | tf_op jit(solution)/shard_map/ppermute | solution.py:245
  133.5 17.6 %collective-permute-start.30 = (f32[128,512]{1,0:T(8,128)S(1)}, f32[128,512]{1,0:T(8,128)S(1)}, u32[]{:S(2)}, u32[]{:S(2)}) collective-permute-start(f32[128,512]{1,0:T(8,128)S(1)} %get-tuple-element.74), channel_id=1, source_target_pairs={{0,28},{4,24},{8,20},{12,16},{16,12},{20,8},{24,4},{28,0},{1,29},{... | collective-permute-start | bytes 786440 | tf_op jit(solution)/shard_map/ppermute | solution.py:245
  (6 other events, 38.7 us)

commit v2 on v1

--- a/solution.py
+++ b/solution.py
@@ -287,11 +287,7 @@
 
 
 def gather_chips(own):
-    parts = lax.axis_size("band")
-    groups = [list(range(core, parts, 2)) for core in range(2)]
-    copies = jnp.broadcast_to(own, (parts // 2, *own.shape))
-    got = lax.all_to_all(copies, "band", 0, 0, axis_index_groups=groups)
-    return got.reshape(-1, own.shape[1])
+    return [own] + [swap(own, "band", 2 * d) for d in range(1, lax.axis_size("band") // 2)]
 
 
 def place_bands(first_ref, parts, flat_ref):
@@ -307,7 +303,7 @@
         core = jnp.bitwise_xor(jnp.bitwise_and(idx_ref[0], 1), c)
         for chip in range(chips):
             for z in range(cuts):
-                at = (core * chips + chip) * cuts
+                at = (core * chips + jnp.bitwise_xor(idx_ref[1], chip)) * cuts
                 at = at + (jnp.bitwise_xor(idx_ref[2], z) if cuts > 1 else 0)
                 start = (chip * cuts + z) * rows
                 flat_ref[pl.ds(pl.multiple_of(at * rows, 8), rows), :] = ref[start : start + rows, :]
@@ -513,6 +509,7 @@
     second = gather_chips(second)
     below, mark = neck_factor(rest, mark, idx)
     second, mark = lax.optimization_barrier((second, mark))
+    second = jnp.concatenate(second, axis=0)
     cuts = lax.axis_size("ga") if lax.axis_size("ga") <= 4 else 1
     result = tail_product(
         top, below, mark, (second, swap(second, "band", 1)), high, low, parts // 2, cuts, idx, head

time: 153 us -> 148 us (0.967)
  local copies, waits for them, and re-layouts: 6.4 us -> 1.85 us
    ppermute x31 -> x34, starting transfers between devices: 35.5 us -> 39.3 us  [swap(): lax.ppermute(x, axis, [(i, i ^ d) for i in range(lax.axis_size(axis))])]
    all_to_all x1 -> x0, starting transfers between devices: 3.68 us -> none  [gather_chips(): got = lax.all_to_all(copies, 'band', 0, 0, axis_index_groups=groups)]
    unnamed x12 -> x3, local copies, waits for them, and re-layouts: 3.68 us -> 0.05 us
    all_to_all x1 -> x0, waiting for transfers between devices: 2.5 us -> none  [gather_chips(): got = lax.all_to_all(copies, 'band', 0, 0, axis_index_groups=groups)]
    ppermute x31 -> x34, waiting for transfers between devices: 56.4 us -> 58 us  [swap(): lax.ppermute(x, axis, [(i, i ^ d) for i in range(lax.axis_size(axis))])]
  transfers between devices with their start and end apart: 32 -> 34, of which waited for: 18 -> 18; matrix products, arithmetic and copies ran while one was open for 0% -> 0% of each run, Pallas kernels for 9% -> 10%
where the time goes in v2:
time: 148 us
  waiting for transfers between devices  58 us (39%)
  starting transfers between devices  39.3 us (27%)
  Pallas kernels  38.5 us (26%)
  blocking collectives  10 us (7%)
  local copies, waits for them, and re-layouts  1.85 us (1%)
    ppermute x34, waiting for transfers between devices, swap(): lax.ppermute(x, axis, [(i, i ^ d) for i in range(lax.axis_size(axis))])  58 us
    ppermute x34, starting transfers between devices, swap(): lax.ppermute(x, axis, [(i, i ^ d) for i in range(lax.axis_size(axis))])  39.3 us
    pallas_call x7, Pallas kernels, vmem_call(): pl.pallas_call(kernel, out_shape=shapes, in_specs=[pl.BlockSpec(memory_sp...  38.5 us
    all_gather x1, blocking collectives, sum_first(): return lax.all_gather(total, 'band', axis=0, tiled=True)  10 us
  transfers between devices with their start and end apart: 34, of which 18 were waited for; matrix products, arithmetic and copies ran while one was open for 0% of the time, Pallas kernels for 10%

profile of v2, /device:TPU:0, one launch (start us, length us, event | category | flops | bytes accessed | tf_op | source)
XLA Modules:
  0.0 147.9 jit_solution(12181757233277790800)
XLA Ops:
  0.0 1.8 %constant_dynamic-slice_fusion = (f32[128,512]{1,0:T(8,128)S(1)}, f32[128,512]{1,0:T(8,128)S(1)}, f32[128,512]{1,0:T(8,128)S(1)}, f32[128,512]{1,0:T(8,128)S(1)}...) fusion(f32[128,4096]{1,0:T(8,128)} %param.1, ...), kind=kLoop, calls=%fused_computation.8 | loop fusion | bytes 4194336 | tf_op jit(solution)/shard_map/dynamic_slice | solution.py:145
  1.8 3.4 %collective-permute-start.6 = (f32[128,512]{1,0:T(8,128)S(1)}, f32[128,512]{1,0:T(8,128)S(1)}, u32[]{:S(2)}, u32[]{:S(2)}) collective-permute-start(f32[128,512]{1,0:T(8,128)S(1)} %get-tuple-element.81), channel_id=1, source_target_pairs={{0,28},{4,24},{8,20},{12,16},{16,12},{20,8},{24,4},{28,0},{1,29},{... | collective-permute-start | bytes 786440 | tf_op jit(solution)/shard_map/ppermute | solution.py:245
  6.0 1.5 %collective-permute-start.3 = (f32[128,512]{1,0:T(8,128)S(1)}, f32[128,512]{1,0:T(8,128)S(1)}, u32[]{:S(2)}, u32[]{:S(2)}) collective-permute-start(f32[128,512]{1,0:T(8,128)S(1)} %get-tuple-element.83), channel_id=1, source_target_pairs={{0,16},{4,20},{8,24},{12,28},{16,0},{20,4},{24,8},{28,12},{1,17},{... | collective-permute-start | bytes 786440 | tf_op jit(solution)/shard_map/ppermute | solution.py:245
  8.7 3.2 %collective-permute-done.6.refs_7_ = f32[128,512]{1,0:T(8,128)S(1)} collective-permute-done((f32[128,512]{1,0:T(8,128)S(1)}, f32[128,512]{1,0:T(8,128)S(1)}, u32[]{:S(2)}, u32[]{:S(2)}) %collective-permute-start.6) | collective-permute-done | bytes 262176 | tf_op jit(solution)/shard_map/ppermute | solution.py:245
  12.8 4.8 %collective-permute-done.4.refs_5_ = f32[128,512]{1,0:T(8,128)S(1)} collective-permute-done((f32[128,512]{1,0:T(8,128)S(1)}, f32[128,512]{1,0:T(8,128)S(1)}, u32[]{:S(2)}, u32[]{:S(2)}) %collective-permute-start.4) | collective-permute-done | bytes 262176 | tf_op jit(solution)/shard_map/ppermute | solution.py:245
  17.6 2.4 %collective-permute-start.5 = (f32[128,512]{1,0:T(8,128)S(1)}, f32[128,512]{1,0:T(8,128)S(1)}, u32[]{:S(2)}, u32[]{:S(2)}) collective-permute-start(f32[128,512]{1,0:T(8,128)S(1)} %get-tuple-element.88), channel_id=1, source_target_pairs={{0,24},{4,28},{8,16},{12,20},{16,8},{20,12},{24,0},{28,4},{1,25},{... | collective-permute-start | bytes 786440 | tf_op jit(solution)/shard_map/ppermute | solution.py:245
  20.1 4.0 %collective-permute-done.3.refs_4_ = f32[128,512]{1,0:T(8,128)S(1)} collective-permute-done((f32[128,512]{1,0:T(8,128)S(1)}, f32[128,512]{1,0:T(8,128)S(1)}, u32[]{:S(2)}, u32[]{:S(2)}) %collective-permute-start.3) | collective-permute-done | bytes 262176 | tf_op jit(solution)/shard_map/ppermute | solution.py:245
  24.2 4.8 %collective-permute-done.5.refs_6_ = f32[128,512]{1,0:T(8,128)S(1)} collective-permute-done((f32[128,512]{1,0:T(8,128)S(1)}, f32[128,512]{1,0:T(8,128)S(1)}, u32[]{:S(2)}, u32[]{:S(2)}) %collective-permute-start.5) | collective-permute-done | bytes 262176 | tf_op jit(solution)/shard_map/ppermute | solution.py:245
  29.0 3.5 %shard_map.17 = (f32[2304,128]{1,0:T(8,128)S(1)}, f32[2304,128]{1,0:T(8,128)S(1)}, bf16[1024,512]{1,0:T(8,128)(2,1)S(1)}, bf16[1024,512]{1,0:T(8,128)(2,1)S(1)}) custom-call(s32[3]{0:T(128)S(1)} %pad_add_fusion.idx_ref, f32[128,512]{1,0:T(8,128)S(1)} %get-tuple-element.87.refs_0_, f32[128,512]{1,0:T(8,128)S(1)} %collective-permute-done.refs_1_, ...), custom_call_target="tpu_custom_call" | custom-call | flops 1000000000 | tf_op jit(solution)/shard_map/pallas_call | solution.py:126
  32.5 2.8 %collective-permute-done.7.refs_1_ = f32[2304,128]{1,0:T(8,128)S(1)} collective-permute-done((f32[2304,128]{1,0:T(8,128)S(1)}, f32[2304,128]{1,0:T(8,128)S(1)}, u32[]{:S(2)}, u32[]{:S(2)}) %collective-permute-start.7) | collective-permute-done | bytes 1179680 | tf_op jit(solution)/shard_map/ppermute | solution.py:245
  36.1 2.3 %collective-permute-start.14 = (f32[160,128]{1,0:T(8,128)S(1)}, f32[160,128]{1,0:T(8,128)S(1)}, u32[]{:S(2)}, u32[]{:S(2)}) collective-permute-start(f32[160,128]{1,0:T(8,128)S(1)} %get-tuple-element.54), channel_id=1, source_target_pairs={{0,8},{4,12},{8,0},{12,4},{16,24},{20,28},{24,16},{28,20},{1,9},{5... | collective-permute-start | bytes 245768 | tf_op jit(solution)/shard_map/ppermute | solution.py:245
  38.4 1.5 %collective-permute-start.15 = (f32[160,128]{1,0:T(8,128)S(1)}, f32[160,128]{1,0:T(8,128)S(1)}, u32[]{:S(2)}, u32[]{:S(2)}) collective-permute-start(f32[160,128]{1,0:T(8,128)S(1)} %get-tuple-element.55), channel_id=1, source_target_pairs={{0,16},{4,20},{8,24},{12,28},{16,0},{20,4},{24,8},{28,12},{1,17},{... | collective-permute-start | bytes 245768 | tf_op jit(solution)/shard_map/ppermute | solution.py:245
  41.1 2.5 %collective-permute-done.15 = f32[160,128]{1,0:T(8,128)S(1)} collective-permute-done((f32[160,128]{1,0:T(8,128)S(1)}, f32[160,128]{1,0:T(8,128)S(1)}, u32[]{:S(2)}, u32[]{:S(2)}) %collective-permute-start.15) | collective-permute-done | bytes 81952 | tf_op jit(solution)/shard_map/ppermute | solution.py:245
  43.7 1.6 %collective-permute-done.16 = f32[160,128]{1,0:T(8,128)S(1)} collective-permute-done((f32[160,128]{1,0:T(8,128)S(1)}, f32[160,128]{1,0:T(8,128)S(1)}, u32[]{:S(2)}, u32[]{:S(2)}) %collective-permute-start.16) | collective-permute-done | bytes 81952 | tf_op jit(solution)/shard_map/ppermute | solution.py:245
  45.3 3.7 %collective-permute-start.19 = (f32[160,128]{1,0:T(8,128)S(1)}, f32[160,128]{1,0:T(8,128)S(1)}, u32[]{:S(2)}, u32[]{:S(2)}) collective-permute-start(f32[160,128]{1,0:T(8,128)S(1)} %add_add_fusion.1), channel_id=1, source_target_pairs={{0,3},{1,2},{2,1},{3,0},{4,7},{5,6},{6,5},{7,4},{8,11},{9,10},{10,... | collective-permute-start | bytes 245768 | tf_op jit(solution)/shard_map/ppermute | solution.py:245
  51.6 1.6 %collective-permute-start.10 = (f32[416,128]{1,0:T(8,128)S(1)}, f32[416,128]{1,0:T(8,128)S(1)}, u32[]{:S(2)}, u32[]{:S(2)}) collective-permute-start(f32[416,128]{1,0:T(8,128)S(1)} %get-tuple-element.48), channel_id=1, source_target_pairs={{0,24},{4,28},{8,16},{12,20},{16,8},{20,12},{24,0},{28,4},{1,25},{... | collective-permute-start | bytes 638984 | tf_op jit(solution)/shard_map/ppermute | solution.py:245
  53.2 1.6 %collective-permute-done.18 = f32[160,128]{1,0:T(8,128)S(1)} collective-permute-done((f32[160,128]{1,0:T(8,128)S(1)}, f32[160,128]{1,0:T(8,128)S(1)}, u32[]{:S(2)}, u32[]{:S(2)}) %collective-permute-start.18) | collective-permute-done | bytes 81952 | tf_op jit(solution)/shard_map/ppermute | solution.py:245
  54.9 2.0 %collective-permute-done.8.refs_1_ = f32[416,128]{1,0:T(8,128)S(1)} collective-permute-done((f32[416,128]{1,0:T(8,128)S(1)}, f32[416,128]{1,0:T(8,128)S(1)}, u32[]{:S(2)}, u32[]{:S(2)}) %collective-permute-start.8) | collective-permute-done | bytes 213024 | tf_op jit(solution)/shard_map/ppermute | solution.py:245
  56.9 2.9 %collective-permute-done.9.refs_2_ = f32[416,128]{1,0:T(8,128)S(1)} collective-permute-done((f32[416,128]{1,0:T(8,128)S(1)}, f32[416,128]{1,0:T(8,128)S(1)}, u32[]{:S(2)}, u32[]{:S(2)}) %collective-permute-start.9) | collective-permute-done | bytes 213024 | tf_op jit(solution)/shard_map/ppermute | solution.py:245
  61.8 2.6 %collective-permute-start.12 = (f32[104,128]{1,0:T(8,128)S(1)}, f32[104,128]{1,0:T(8,128)S(1)}, u32[]{:S(2)}, u32[]{:S(2)}) collective-permute-start(f32[104,128]{1,0:T(8,128)S(1)} %get-tuple-element.51), channel_id=1, source_target_pairs={{0,2},{1,3},{2,0},{3,1},{4,6},{5,7},{6,4},{7,5},{8,10},{9,11},{10,... | collective-permute-start | bytes 159752 | tf_op jit(solution)/shard_map/ppermute | solution.py:245
  64.8 10.0 %all_gather.3.first_ref = f32[1280,128]{1,0:T(8,128)S(1)} all-gather(f32[160,128]{1,0:T(8,128)S(1)} %add_add_fusion), channel_id=1, replica_groups=mesh['band'=8,'ga'=4] {'band'}, dimensions={0}, use_global_device_ids=true | all-gather | bytes 737280 | tf_op jit(solution)/shard_map/all_gather | solution.py:271
  74.9 3.5 %collective-permute-start.22 = (f32[104,128]{1,0:T(8,128)S(1)}, f32[104,128]{1,0:T(8,128)S(1)}, u32[]{:S(2)}, u32[]{:S(2)}) collective-permute-start(f32[104,128]{1,0:T(8,128)S(1)} %add_add_fusion.2), channel_id=1, source_target_pairs={{0,3},{1,2},{2,1},{3,0},{4,7},{5,6},{6,5},{7,4},{8,11},{9,10},{10,... | collective-permute-start | bytes 159752 | tf_op jit(solution)/shard_map/ppermute | solution.py:245
  79.4 7.4 %shard_map.20 = (f32[256,256]{1,0:T(8,128)S(1)}, f32[256,512]{1,0:T(8,128)S(1)}, f32[8,128]{1,0:T(8,128)S(1)}) custom-call(s32[3]{0:T(128)S(1)} %pad_add_fusion.idx_ref, f32[1280,128]{1,0:T(8,128)S(1)} %all_gather.3.first_ref), custom_call_target="tpu_custom_call" | custom-call | flops 3000000000 | tf_op jit(solution)/shard_map/pallas_call | solution.py:126
  86.9 1.5 %collective-permute-start.25 = (f32[416,128]{1,0:T(8,128)S(1)}, f32[416,128]{1,0:T(8,128)S(1)}, u32[]{:S(2)}, u32[]{:S(2)}) collective-permute-start(f32[416,128]{1,0:T(8,128)S(1)} %pad_maximum_fusion), channel_id=1, source_target_pairs={{0,24},{4,28},{8,16},{12,20},{16,8},{20,12},{24,0},{28,4},{1,25},{... | collective-permute-start | bytes 638984 | tf_op jit(solution)/shard_map/ppermute | solution.py:245
  90.4 6.9 %shard_map.21 = (f32[256,512]{1,0:T(8,128)S(1)}, f32[8,128]{1,0:T(8,128)S(1)}) custom-call(s32[3]{0:T(128)S(1)} %pad_add_fusion.idx_ref, f32[256,512]{1,0:T(8,128)S(1)} %get-tuple-element.59.in_ref, f32[8,128]{1,0:T(8,128)S(1)} %get-tuple-element.62.before_ref), custom_call_target="tpu_custom_call" | custom-call | flops 3000000000 | tf_op jit(solution)/shard_map/pallas_call | solution.py:126
  97.3 1.7 %collective-permute-done.24 = f32[416,128]{1,0:T(8,128)S(1)} collective-permute-done((f32[416,128]{1,0:T(8,128)S(1)}, f32[416,128]{1,0:T(8,128)S(1)}, u32[]{:S(2)}, u32[]{:S(2)}) %collective-permute-start.24) | collective-permute-done | bytes 213024 | tf_op jit(solution)/shard_map/ppermute | solution.py:245
  99.2 2.4 %collective-permute-done.26.far_ref = f32[1664,128]{1,0:T(8,128)S(1)} collective-permute-done((f32[1664,128]{1,0:T(8,128)S(1)}, f32[1664,128]{1,0:T(8,128)S(1)}, u32[]{:S(2)}, u32[]{:S(2)}) %collective-permute-start.26) | collective-permute-done | bytes 852000 | tf_op jit(solution)/shard_map/ppermute | solution.py:245
  101.6 17.3 %shard_map.22 = (f32[128,512]{1,0:T(8,128)S(1)}, f32[128,512]{1,0:T(8,128)S(1)}, f32[128,512]{1,0:T(8,128)S(1)}, f32[128,512]{1,0:T(8,128)S(1)}, f32[128,512]{1,...) custom-call(s32[3]{0:T(128)S(1)} %pad_add_fusion.idx_ref, ...), custom_call_target="tpu_custom_call" | custom-call | flops 24999999488 | tf_op jit(solution)/shard_map/pallas_call | solution.py:126
  124.1 4.1 %collective-permute-done.28.refs_2_ = f32[128,512]{1,0:T(8,128)S(1)} collective-permute-done((f32[128,512]{1,0:T(8,128)S(1)}, f32[128,512]{1,0:T(8,128)S(1)}, u32[]{:S(2)}, u32[]{:S(2)}) %collective-permute-start.28) | collective-permute-done | bytes 262176 | tf_op jit(solution)/shard_map/ppermute | solution.py:245
  128.4 4.4 %collective-permute-done.29.refs_3_ = f32[128,512]{1,0:T(8,128)S(1)} collective-permute-done((f32[128,512]{1,0:T(8,128)S(1)}, f32[128,512]{1,0:T(8,128)S(1)}, u32[]{:S(2)}, u32[]{:S(2)}) %collective-permute-start.29) | collective-permute-done | bytes 262176 | tf_op jit(solution)/shard_map/ppermute | solution.py:245
  132.8 13.1 %collective-permute-done.31.refs_5_ = f32[128,512]{1,0:T(8,128)S(1)} collective-permute-done((f32[128,512]{1,0:T(8,128)S(1)}, f32[128,512]{1,0:T(8,128)S(1)}, u32[]{:S(2)}, u32[]{:S(2)}) %collective-permute-start.31) | collective-permute-done | bytes 262176 | tf_op jit(solution)/shard_map/ppermute | solution.py:245
  145.9 2.0 %shard_map.23 = f32[128,4096]{1,0:T(8,128)} custom-call(s32[3]{0:T(128)S(1)} %pad_add_fusion.idx_ref, f32[128,512]{1,0:T(8,128)S(1)} %get-tuple-element.73.refs_0_, f32[128,512]{1,0:T(8,128)S(1)} %collective-permute-done.27.refs_1_, f32[128,512]{1,0:T(8,128)S(1)} %collective-permute-done.28.refs_2_, f32[128,512]{1,0:T(8,128)S(1)} %collective-permute-done.29.refs_3_, ...), custom_call_target="tpu_custom_call" | custom-call | flops 1000000000 | tf_op jit(solution)/shard_map/pallas_call | solution.py:126
  (54 shorter events, 18.6 us)
Async XLA Ops:
  1.8 10.1 %collective-permute-start.6 = (f32[128,512]{1,0:T(8,128)S(1)}, f32[128,512]{1,0:T(8,128)S(1)}, u32[]{:S(2)}, u32[]{:S(2)}) collective-permute-start(f32[128,512]{1,0:T(8,128)S(1)} %get-tuple-element.81), channel_id=1, source_target_pairs={{0,28},{4,24},{8,20},{12,16},{16,12},{20,8},{24,4},{28,0},{1,29},{... | collective-permute-start | bytes 786440 | tf_op jit(solution)/shard_map/ppermute | solution.py:245
  5.2 12.4 %collective-permute-start.4 = (f32[128,512]{1,0:T(8,128)S(1)}, f32[128,512]{1,0:T(8,128)S(1)}, u32[]{:S(2)}, u32[]{:S(2)}) collective-permute-start(f32[128,512]{1,0:T(8,128)S(1)} %get-tuple-element.82), channel_id=1, source_target_pairs={{0,20},{4,16},{8,28},{12,24},{16,4},{20,0},{24,12},{28,8},{1,21},{... | collective-permute-start | bytes 786440 | tf_op jit(solution)/shard_map/ppermute | solution.py:245
  6.0 18.1 %collective-permute-start.3 = (f32[128,512]{1,0:T(8,128)S(1)}, f32[128,512]{1,0:T(8,128)S(1)}, u32[]{:S(2)}, u32[]{:S(2)}) collective-permute-start(f32[128,512]{1,0:T(8,128)S(1)} %get-tuple-element.83), channel_id=1, source_target_pairs={{0,16},{4,20},{8,24},{12,28},{16,0},{20,4},{24,8},{28,12},{1,17},{... | collective-permute-start | bytes 786440 | tf_op jit(solution)/shard_map/ppermute | solution.py:245
  7.5 16.6 %collective-permute-start.2 = (f32[128,512]{1,0:T(8,128)S(1)}, f32[128,512]{1,0:T(8,128)S(1)}, u32[]{:S(2)}, u32[]{:S(2)}) collective-permute-start(f32[128,512]{1,0:T(8,128)S(1)} %get-tuple-element.84), channel_id=1, source_target_pairs={{0,12},{4,8},{8,4},{12,0},{16,28},{20,24},{24,20},{28,16},{1,13},{... | collective-permute-start | bytes 786440 | tf_op jit(solution)/shard_map/ppermute | solution.py:245
  7.5 16.7 %collective-permute-start.1 = (f32[128,512]{1,0:T(8,128)S(1)}, f32[128,512]{1,0:T(8,128)S(1)}, u32[]{:S(2)}, u32[]{:S(2)}) collective-permute-start(f32[128,512]{1,0:T(8,128)S(1)} %get-tuple-element.85), channel_id=1, source_target_pairs={{0,8},{4,12},{8,0},{12,4},{16,24},{20,28},{24,16},{28,20},{1,9},{5... | collective-permute-start | bytes 786440 | tf_op jit(solution)/shard_map/ppermute | solution.py:245
  11.9 12.2 %collective-permute-start = (f32[128,512]{1,0:T(8,128)S(1)}, f32[128,512]{1,0:T(8,128)S(1)}, u32[]{:S(2)}, u32[]{:S(2)}) collective-permute-start(f32[128,512]{1,0:T(8,128)S(1)} %get-tuple-element.86), channel_id=1, source_target_pairs={{0,4},{4,0},{8,12},{12,8},{16,20},{20,16},{24,28},{28,24},{1,5},{5... | collective-permute-start | bytes 786440 | tf_op jit(solution)/shard_map/ppermute | solution.py:245
  17.6 11.4 %collective-permute-start.5 = (f32[128,512]{1,0:T(8,128)S(1)}, f32[128,512]{1,0:T(8,128)S(1)}, u32[]{:S(2)}, u32[]{:S(2)}) collective-permute-start(f32[128,512]{1,0:T(8,128)S(1)} %get-tuple-element.88), channel_id=1, source_target_pairs={{0,24},{4,28},{8,16},{12,20},{16,8},{20,12},{24,0},{28,4},{1,25},{... | collective-permute-start | bytes 786440 | tf_op jit(solution)/shard_map/ppermute | solution.py:245
  36.1 5.1 %collective-permute-start.14 = (f32[160,128]{1,0:T(8,128)S(1)}, f32[160,128]{1,0:T(8,128)S(1)}, u32[]{:S(2)}, u32[]{:S(2)}) collective-permute-start(f32[160,128]{1,0:T(8,128)S(1)} %get-tuple-element.54), channel_id=1, source_target_pairs={{0,8},{4,12},{8,0},{12,4},{16,24},{20,28},{24,16},{28,20},{1,9},{5... | collective-permute-start | bytes 245768 | tf_op jit(solution)/shard_map/ppermute | solution.py:245
  38.4 5.3 %collective-permute-start.15 = (f32[160,128]{1,0:T(8,128)S(1)}, f32[160,128]{1,0:T(8,128)S(1)}, u32[]{:S(2)}, u32[]{:S(2)}) collective-permute-start(f32[160,128]{1,0:T(8,128)S(1)} %get-tuple-element.55), channel_id=1, source_target_pairs={{0,16},{4,20},{8,24},{12,28},{16,0},{20,4},{24,8},{28,12},{1,17},{... | collective-permute-start | bytes 245768 | tf_op jit(solution)/shard_map/ppermute | solution.py:245
  39.9 5.3 %collective-permute-start.16 = (f32[160,128]{1,0:T(8,128)S(1)}, f32[160,128]{1,0:T(8,128)S(1)}, u32[]{:S(2)}, u32[]{:S(2)}) collective-permute-start(f32[160,128]{1,0:T(8,128)S(1)} %get-tuple-element.56), channel_id=1, source_target_pairs={{0,24},{4,28},{8,16},{12,20},{16,8},{20,12},{24,0},{28,4},{1,25},{... | collective-permute-start | bytes 245768 | tf_op jit(solution)/shard_map/ppermute | solution.py:245
  45.3 6.3 %collective-permute-start.19 = (f32[160,128]{1,0:T(8,128)S(1)}, f32[160,128]{1,0:T(8,128)S(1)}, u32[]{:S(2)}, u32[]{:S(2)}) collective-permute-start(f32[160,128]{1,0:T(8,128)S(1)} %add_add_fusion.1), channel_id=1, source_target_pairs={{0,3},{1,2},{2,1},{3,0},{4,7},{5,6},{6,5},{7,4},{8,11},{9,10},{10,... | collective-permute-start | bytes 245768 | tf_op jit(solution)/shard_map/ppermute | solution.py:245
  48.9 5.9 %collective-permute-start.18 = (f32[160,128]{1,0:T(8,128)S(1)}, f32[160,128]{1,0:T(8,128)S(1)}, u32[]{:S(2)}, u32[]{:S(2)}) collective-permute-start(f32[160,128]{1,0:T(8,128)S(1)} %add_add_fusion.1), channel_id=1, source_target_pairs={{0,2},{1,3},{2,0},{3,1},{4,6},{5,7},{6,4},{7,5},{8,10},{9,11},{10,... | collective-permute-start | bytes 245768 | tf_op jit(solution)/shard_map/ppermute | solution.py:245
  48.9 5.9 %collective-permute-start.17 = (f32[160,128]{1,0:T(8,128)S(1)}, f32[160,128]{1,0:T(8,128)S(1)}, u32[]{:S(2)}, u32[]{:S(2)}) collective-permute-start(f32[160,128]{1,0:T(8,128)S(1)} %add_add_fusion.1), channel_id=1, source_target_pairs={{0,1},{1,0},{2,3},{3,2},{4,5},{5,4},{6,7},{7,6},{8,9},{9,8},{10,11... | collective-permute-start | bytes 245768 | tf_op jit(solution)/shard_map/ppermute | solution.py:245
  49.7 7.2 %collective-permute-start.8 = (f32[416,128]{1,0:T(8,128)S(1)}, f32[416,128]{1,0:T(8,128)S(1)}, u32[]{:S(2)}, u32[]{:S(2)}) collective-permute-start(f32[416,128]{1,0:T(8,128)S(1)} %get-tuple-element.46), channel_id=1, source_target_pairs={{0,8},{4,12},{8,0},{12,4},{16,24},{20,28},{24,16},{28,20},{1,9},{5... | collective-permute-start | bytes 638984 | tf_op jit(solution)/shard_map/ppermute | solution.py:245
  50.3 9.5 %collective-permute-start.9 = (f32[416,128]{1,0:T(8,128)S(1)}, f32[416,128]{1,0:T(8,128)S(1)}, u32[]{:S(2)}, u32[]{:S(2)}) collective-permute-start(f32[416,128]{1,0:T(8,128)S(1)} %get-tuple-element.47), channel_id=1, source_target_pairs={{0,16},{4,20},{8,24},{12,28},{16,0},{20,4},{24,8},{28,12},{1,17},{... | collective-permute-start | bytes 638984 | tf_op jit(solution)/shard_map/ppermute | solution.py:245
  51.6 8.2 %collective-permute-start.10 = (f32[416,128]{1,0:T(8,128)S(1)}, f32[416,128]{1,0:T(8,128)S(1)}, u32[]{:S(2)}, u32[]{:S(2)}) collective-permute-start(f32[416,128]{1,0:T(8,128)S(1)} %get-tuple-element.48), channel_id=1, source_target_pairs={{0,24},{4,28},{8,16},{12,20},{16,8},{20,12},{24,0},{28,4},{1,25},{... | collective-permute-start | bytes 638984 | tf_op jit(solution)/shard_map/ppermute | solution.py:245
  60.4 14.5 %collective-permute-start.11 = (f32[104,128]{1,0:T(8,128)S(1)}, f32[104,128]{1,0:T(8,128)S(1)}, u32[]{:S(2)}, u32[]{:S(2)}) collective-permute-start(f32[104,128]{1,0:T(8,128)S(1)} %get-tuple-element.50), channel_id=1, source_target_pairs={{0,1},{1,0},{2,3},{3,2},{4,5},{5,4},{6,7},{7,6},{8,9},{9,8},{10,11... | collective-permute-start | bytes 159752 | tf_op jit(solution)/shard_map/ppermute | solution.py:245
  61.8 13.1 %collective-permute-start.12 = (f32[104,128]{1,0:T(8,128)S(1)}, f32[104,128]{1,0:T(8,128)S(1)}, u32[]{:S(2)}, u32[]{:S(2)}) collective-permute-start(f32[104,128]{1,0:T(8,128)S(1)} %get-tuple-element.51), channel_id=1, source_target_pairs={{0,2},{1,3},{2,0},{3,1},{4,6},{5,7},{6,4},{7,5},{8,10},{9,11},{10,... | collective-permute-start | bytes 159752 | tf_op jit(solution)/shard_map/ppermute | solution.py:245
  64.4 10.4 %collective-permute-start.13 = (f32[104,128]{1,0:T(8,128)S(1)}, f32[104,128]{1,0:T(8,128)S(1)}, u32[]{:S(2)}, u32[]{:S(2)}) collective-permute-start(f32[104,128]{1,0:T(8,128)S(1)} %get-tuple-element.52), channel_id=1, source_target_pairs={{0,3},{1,2},{2,1},{3,0},{4,7},{5,6},{6,5},{7,4},{8,11},{9,10},{10,... | collective-permute-start | bytes 159752 | tf_op jit(solution)/shard_map/ppermute | solution.py:245
  74.9 11.9 %collective-permute-start.22 = (f32[104,128]{1,0:T(8,128)S(1)}, f32[104,128]{1,0:T(8,128)S(1)}, u32[]{:S(2)}, u32[]{:S(2)}) collective-permute-start(f32[104,128]{1,0:T(8,128)S(1)} %add_add_fusion.2), channel_id=1, source_target_pairs={{0,3},{1,2},{2,1},{3,0},{4,7},{5,6},{6,5},{7,4},{8,11},{9,10},{10,... | collective-permute-start | bytes 159752 | tf_op jit(solution)/shard_map/ppermute | solution.py:245
  78.4 8.5 %collective-permute-start.21 = (f32[104,128]{1,0:T(8,128)S(1)}, f32[104,128]{1,0:T(8,128)S(1)}, u32[]{:S(2)}, u32[]{:S(2)}) collective-permute-start(f32[104,128]{1,0:T(8,128)S(1)} %add_add_fusion.2), channel_id=1, source_target_pairs={{0,2},{1,3},{2,0},{3,1},{4,6},{5,7},{6,4},{7,5},{8,10},{9,11},{10,... | collective-permute-start | bytes 159752 | tf_op jit(solution)/shard_map/ppermute | solution.py:245
  78.4 8.5 %collective-permute-start.20 = (f32[104,128]{1,0:T(8,128)S(1)}, f32[104,128]{1,0:T(8,128)S(1)}, u32[]{:S(2)}, u32[]{:S(2)}) collective-permute-start(f32[104,128]{1,0:T(8,128)S(1)} %add_add_fusion.2), channel_id=1, source_target_pairs={{0,1},{1,0},{2,3},{3,2},{4,5},{5,4},{6,7},{7,6},{8,9},{9,8},{10,11... | collective-permute-start | bytes 159752 | tf_op jit(solution)/shard_map/ppermute | solution.py:245
  86.9 10.5 %collective-permute-start.25 = (f32[416,128]{1,0:T(8,128)S(1)}, f32[416,128]{1,0:T(8,128)S(1)}, u32[]{:S(2)}, u32[]{:S(2)}) collective-permute-start(f32[416,128]{1,0:T(8,128)S(1)} %pad_maximum_fusion), channel_id=1, source_target_pairs={{0,24},{4,28},{8,16},{12,20},{16,8},{20,12},{24,0},{28,4},{1,25},{... | collective-permute-start | bytes 638984 | tf_op jit(solution)/shard_map/ppermute | solution.py:245
  88.4 10.7 %collective-permute-start.24 = (f32[416,128]{1,0:T(8,128)S(1)}, f32[416,128]{1,0:T(8,128)S(1)}, u32[]{:S(2)}, u32[]{:S(2)}) collective-permute-start(f32[416,128]{1,0:T(8,128)S(1)} %pad_maximum_fusion), channel_id=1, source_target_pairs={{0,16},{4,20},{8,24},{12,28},{16,0},{20,4},{24,8},{28,12},{1,17},{... | collective-permute-start | bytes 638984 | tf_op jit(solution)/shard_map/ppermute | solution.py:245
  89.3 9.8 %collective-permute-start.23 = (f32[416,128]{1,0:T(8,128)S(1)}, f32[416,128]{1,0:T(8,128)S(1)}, u32[]{:S(2)}, u32[]{:S(2)}) collective-permute-start(f32[416,128]{1,0:T(8,128)S(1)} %pad_maximum_fusion), channel_id=1, source_target_pairs={{0,8},{4,12},{8,0},{12,4},{16,24},{20,28},{24,16},{28,20},{1,9},{5... | collective-permute-start | bytes 638984 | tf_op jit(solution)/shard_map/ppermute | solution.py:245
  118.9 3.7 %collective-permute-start.27 = (f32[128,512]{1,0:T(8,128)S(1)}, f32[128,512]{1,0:T(8,128)S(1)}, u32[]{:S(2)}, u32[]{:S(2)}) collective-permute-start(f32[128,512]{1,0:T(8,128)S(1)} %get-tuple-element.74), channel_id=1, source_target_pairs={{0,4},{4,0},{8,12},{12,8},{16,20},{20,16},{24,28},{28,24},{1,5},{5... | collective-permute-start | bytes 786440 | tf_op jit(solution)/shard_map/ppermute | solution.py:245
  119.2 9.1 %collective-permute-start.28 = (f32[128,512]{1,0:T(8,128)S(1)}, f32[128,512]{1,0:T(8,128)S(1)}, u32[]{:S(2)}, u32[]{:S(2)}) collective-permute-start(f32[128,512]{1,0:T(8,128)S(1)} %get-tuple-element.75), channel_id=1, source_target_pairs={{0,8},{4,12},{8,0},{12,4},{16,24},{20,28},{24,16},{28,20},{1,9},{5... | collective-permute-start | bytes 786440 | tf_op jit(solution)/shard_map/ppermute | solution.py:245
  120.1 12.7 %collective-permute-start.29 = (f32[128,512]{1,0:T(8,128)S(1)}, f32[128,512]{1,0:T(8,128)S(1)}, u32[]{:S(2)}, u32[]{:S(2)}) collective-permute-start(f32[128,512]{1,0:T(8,128)S(1)} %get-tuple-element.76), channel_id=1, source_target_pairs={{0,12},{4,8},{8,4},{12,0},{16,28},{20,24},{24,20},{28,16},{1,13},{... | collective-permute-start | bytes 786440 | tf_op jit(solution)/shard_map/ppermute | solution.py:245
  120.9 11.9 %collective-permute-start.30 = (f32[128,512]{1,0:T(8,128)S(1)}, f32[128,512]{1,0:T(8,128)S(1)}, u32[]{:S(2)}, u32[]{:S(2)}) collective-permute-start(f32[128,512]{1,0:T(8,128)S(1)} %get-tuple-element.77), channel_id=1, source_target_pairs={{0,16},{4,20},{8,24},{12,28},{16,0},{20,4},{24,8},{28,12},{1,17},{... | collective-permute-start | bytes 786440 | tf_op jit(solution)/shard_map/ppermute | solution.py:245
  121.8 24.2 %collective-permute-start.31 = (f32[128,512]{1,0:T(8,128)S(1)}, f32[128,512]{1,0:T(8,128)S(1)}, u32[]{:S(2)}, u32[]{:S(2)}) collective-permute-start(f32[128,512]{1,0:T(8,128)S(1)} %get-tuple-element.78), channel_id=1, source_target_pairs={{0,20},{4,16},{8,28},{12,24},{16,4},{20,0},{24,12},{28,8},{1,21},{... | collective-permute-start | bytes 786440 | tf_op jit(solution)/shard_map/ppermute | solution.py:245
  122.7 23.3 %collective-permute-start.32 = (f32[128,512]{1,0:T(8,128)S(1)}, f32[128,512]{1,0:T(8,128)S(1)}, u32[]{:S(2)}, u32[]{:S(2)}) collective-permute-start(f32[128,512]{1,0:T(8,128)S(1)} %get-tuple-element.79), channel_id=1, source_target_pairs={{0,24},{4,28},{8,16},{12,20},{16,8},{20,12},{24,0},{28,4},{1,25},{... | collective-permute-start | bytes 786440 | tf_op jit(solution)/shard_map/ppermute | solution.py:245
  128.3 17.6 %collective-permute-start.33 = (f32[128,512]{1,0:T(8,128)S(1)}, f32[128,512]{1,0:T(8,128)S(1)}, u32[]{:S(2)}, u32[]{:S(2)}) collective-permute-start(f32[128,512]{1,0:T(8,128)S(1)} %get-tuple-element.80), channel_id=1, source_target_pairs={{0,28},{4,24},{8,20},{12,16},{16,12},{20,8},{24,4},{28,0},{1,29},{... | collective-permute-start | bytes 786440 | tf_op jit(solution)/shard_map/ppermute | solution.py:245
  (2 other events, 5.4 us)

commit v3 on v2

--- a/solution.py
+++ b/solution.py
@@ -145,18 +145,40 @@
     return [lax.dynamic_slice_in_dim(x, (band ^ d) * width, width, 1) for d in range(parts)]
 
 
-def join_kernel(parts, width, idx_ref, *refs):
-    for d in range(parts):
+def join_kernel(offsets, width, idx_ref, *refs):
+    pieces, out_ref, sems = refs[: len(offsets)], refs[-2], refs[-1]
+    copies = []
+    for n, d in enumerate(offsets):
         start = pl.multiple_of(jnp.bitwise_xor(idx_ref[0], d) * width, width)
-        refs[parts][:, pl.ds(start, width)] = refs[d][...]
+        copies.append(
+            pltpu.make_async_copy(pieces[n], out_ref.at[:, pl.ds(start, width)], sems.at[n])
+        )
+    for copy in copies:
+        copy.start()
+    for copy in copies:
+        copy.wait()
 
 
 def join_columns(pieces, idx):
     parts = len(pieces)
     rows, width = pieces[0].shape
-    return vmem_call(
-        functools.partial(join_kernel, parts, width), [f32(rows, width * parts)], [], idx, pieces, vmem=8
-    )[0]
+    out = []
+    vmem, anywhere = pl.BlockSpec(memory_space=pltpu.VMEM), pl.BlockSpec(memory_space=pl.ANY)
+    for offsets in (range(parts // 2), range(parts // 2, parts)):
+        out = [
+            pl.pallas_call(
+                functools.partial(join_kernel, offsets, width),
+                out_shape=f32(rows, width * parts),
+                in_specs=[pl.BlockSpec(memory_space=pltpu.SMEM)]
+                + [vmem] * len(offsets)
+                + [anywhere] * len(out),
+                out_specs=anywhere,
+                scratch_shapes=[pltpu.SemaphoreType.DMA((len(offsets),))],
+                input_output_aliases={1 + len(offsets): 0} if out else {},
+                compiler_params=pltpu.CompilerParams(vmem_limit_bytes=8 * 2**20),
+            )(idx, *[pieces[d] for d in offsets], *out)
+        ]
+    return out[0]
 
 
 def sum_split_kernel(terms, sections, parts, slot, idx_ref, *refs):

time: 148 us -> 146 us (0.986)
  waiting for transfers between devices: 58 us -> 54.7 us
    ppermute x34, waiting for transfers between devices: 58 us -> 54.7 us  [swap(): lax.ppermute(x, axis, [(i, i ^ d) for i in range(lax.axis_size(axis))])]
    pallas_call x0 -> x2, Pallas kernels: none -> 3.08 us  [join_columns(): pl.pallas_call(functools.partial(join_kernel, offsets, width), out_shape=...]
    pallas_call x7 -> x6, Pallas kernels: 38.5 us -> 36.5 us  [vmem_call(): pl.pallas_call(kernel, out_shape=shapes, in_specs=[pl.BlockSpec(memory_sp...]
  transfers between devices with their start and end apart: 34 -> 34, of which waited for: 18 -> 19; matrix products, arithmetic and copies ran while one was open for 0% -> 0% of each run, Pallas kernels for 10% -> 11%
where the time goes in v3:
time: 146 us
  waiting for transfers between devices  54.7 us (37%)
  Pallas kernels  39.6 us (27%)
  starting transfers between devices  39.5 us (27%)
  blocking collectives  10 us (7%)
  local copies, waits for them, and re-layouts  1.85 us (1%)
    ppermute x34, waiting for transfers between devices, swap(): lax.ppermute(x, axis, [(i, i ^ d) for i in range(lax.axis_size(axis))])  54.7 us
    ppermute x34, starting transfers between devices, swap(): lax.ppermute(x, axis, [(i, i ^ d) for i in range(lax.axis_size(axis))])  39.5 us
    pallas_call x6, Pallas kernels, vmem_call(): pl.pallas_call(kernel, out_shape=shapes, in_specs=[pl.BlockSpec(memory_sp...  36.5 us
    all_gather x1, blocking collectives, sum_first(): return lax.all_gather(total, 'band', axis=0, tiled=True)  10 us
    pallas_call x2, Pallas kernels, join_columns(): pl.pallas_call(functools.partial(join_kernel, offsets, width), out_shape=...  3.08 us
  transfers between devices with their start and end apart: 34, of which 19 were waited for; matrix products, arithmetic and copies ran while one was open for 0% of the time, Pallas kernels for 11%

profile of v3, /device:TPU:0, one launch (start us, length us, event | category | flops | bytes accessed | tf_op | source)
XLA Modules:
  0.0 146.2 jit_solution(1608576378284876167)
XLA Ops:
  0.0 1.8 %constant_dynamic-slice_fusion = (f32[128,512]{1,0:T(8,128)S(1)}, f32[128,512]{1,0:T(8,128)S(1)}, f32[128,512]{1,0:T(8,128)S(1)}, f32[128,512]{1,0:T(8,128)S(1)}...) fusion(f32[128,4096]{1,0:T(8,128)} %param.1, ...), kind=kLoop, calls=%fused_computation.8 | loop fusion | bytes 4194336 | tf_op jit(solution)/shard_map/dynamic_slice | solution.py:145
  1.8 3.4 %collective-permute-start.6 = (f32[128,512]{1,0:T(8,128)S(1)}, f32[128,512]{1,0:T(8,128)S(1)}, u32[]{:S(2)}, u32[]{:S(2)}) collective-permute-start(f32[128,512]{1,0:T(8,128)S(1)} %get-tuple-element.81), channel_id=1, source_target_pairs={{0,28},{4,24},{8,20},{12,16},{16,12},{20,8},{24,4},{28,0},{1,29},{... | collective-permute-start | bytes 786440 | tf_op jit(solution)/shard_map/ppermute | solution.py:267
  8.7 3.2 %collective-permute-done.6.refs_7_ = f32[128,512]{1,0:T(8,128)S(1)} collective-permute-done((f32[128,512]{1,0:T(8,128)S(1)}, f32[128,512]{1,0:T(8,128)S(1)}, u32[]{:S(2)}, u32[]{:S(2)}) %collective-permute-start.6) | collective-permute-done | bytes 262176 | tf_op jit(solution)/shard_map/ppermute | solution.py:267
  12.8 4.8 %collective-permute-done.4.refs_5_ = f32[128,512]{1,0:T(8,128)S(1)} collective-permute-done((f32[128,512]{1,0:T(8,128)S(1)}, f32[128,512]{1,0:T(8,128)S(1)}, u32[]{:S(2)}, u32[]{:S(2)}) %collective-permute-start.4) | collective-permute-done | bytes 262176 | tf_op jit(solution)/shard_map/ppermute | solution.py:267
  17.6 2.4 %collective-permute-start.5 = (f32[128,512]{1,0:T(8,128)S(1)}, f32[128,512]{1,0:T(8,128)S(1)}, u32[]{:S(2)}, u32[]{:S(2)}) collective-permute-start(f32[128,512]{1,0:T(8,128)S(1)} %get-tuple-element.88), channel_id=1, source_target_pairs={{0,24},{4,28},{8,16},{12,20},{16,8},{20,12},{24,0},{28,4},{1,25},{... | collective-permute-start | bytes 786440 | tf_op jit(solution)/shard_map/ppermute | solution.py:267
  20.1 4.0 %collective-permute-done.3.refs_4_ = f32[128,512]{1,0:T(8,128)S(1)} collective-permute-done((f32[128,512]{1,0:T(8,128)S(1)}, f32[128,512]{1,0:T(8,128)S(1)}, u32[]{:S(2)}, u32[]{:S(2)}) %collective-permute-start.3) | collective-permute-done | bytes 262176 | tf_op jit(solution)/shard_map/ppermute | solution.py:267
  24.2 4.8 %collective-permute-done.5.refs_6_ = f32[128,512]{1,0:T(8,128)S(1)} collective-permute-done((f32[128,512]{1,0:T(8,128)S(1)}, f32[128,512]{1,0:T(8,128)S(1)}, u32[]{:S(2)}, u32[]{:S(2)}) %collective-permute-start.5) | collective-permute-done | bytes 262176 | tf_op jit(solution)/shard_map/ppermute | solution.py:267
  29.0 3.5 %shard_map.17 = (f32[2304,128]{1,0:T(8,128)S(1)}, f32[2304,128]{1,0:T(8,128)S(1)}, bf16[1024,512]{1,0:T(8,128)(2,1)S(1)}, bf16[1024,512]{1,0:T(8,128)(2,1)S(1)}) custom-call(s32[3]{0:T(128)S(1)} %pad_add_fusion.idx_ref, f32[128,512]{1,0:T(8,128)S(1)} %get-tuple-element.87.refs_0_, f32[128,512]{1,0:T(8,128)S(1)} %collective-permute-done.refs_1_, ...), custom_call_target="tpu_custom_call" | custom-call | flops 1000000000 | tf_op jit(solution)/shard_map/pallas_call | solution.py:126
  32.5 2.8 %collective-permute-done.7.refs_1_ = f32[2304,128]{1,0:T(8,128)S(1)} collective-permute-done((f32[2304,128]{1,0:T(8,128)S(1)}, f32[2304,128]{1,0:T(8,128)S(1)}, u32[]{:S(2)}, u32[]{:S(2)}) %collective-permute-start.7) | collective-permute-done | bytes 1179680 | tf_op jit(solution)/shard_map/ppermute | solution.py:267
  36.1 2.3 %collective-permute-start.14 = (f32[160,128]{1,0:T(8,128)S(1)}, f32[160,128]{1,0:T(8,128)S(1)}, u32[]{:S(2)}, u32[]{:S(2)}) collective-permute-start(f32[160,128]{1,0:T(8,128)S(1)} %get-tuple-element.54), channel_id=1, source_target_pairs={{0,8},{4,12},{8,0},{12,4},{16,24},{20,28},{24,16},{28,20},{1,9},{5... | collective-permute-start | bytes 245768 | tf_op jit(solution)/shard_map/ppermute | solution.py:267
  38.4 1.5 %collective-permute-start.15 = (f32[160,128]{1,0:T(8,128)S(1)}, f32[160,128]{1,0:T(8,128)S(1)}, u32[]{:S(2)}, u32[]{:S(2)}) collective-permute-start(f32[160,128]{1,0:T(8,128)S(1)} %get-tuple-element.55), channel_id=1, source_target_pairs={{0,16},{4,20},{8,24},{12,28},{16,0},{20,4},{24,8},{28,12},{1,17},{... | collective-permute-start | bytes 245768 | tf_op jit(solution)/shard_map/ppermute | solution.py:267
  41.1 2.5 %collective-permute-done.15 = f32[160,128]{1,0:T(8,128)S(1)} collective-permute-done((f32[160,128]{1,0:T(8,128)S(1)}, f32[160,128]{1,0:T(8,128)S(1)}, u32[]{:S(2)}, u32[]{:S(2)}) %collective-permute-start.15) | collective-permute-done | bytes 81952 | tf_op jit(solution)/shard_map/ppermute | solution.py:267
  43.7 1.6 %collective-permute-done.16 = f32[160,128]{1,0:T(8,128)S(1)} collective-permute-done((f32[160,128]{1,0:T(8,128)S(1)}, f32[160,128]{1,0:T(8,128)S(1)}, u32[]{:S(2)}, u32[]{:S(2)}) %collective-permute-start.16) | collective-permute-done | bytes 81952 | tf_op jit(solution)/shard_map/ppermute | solution.py:267
  45.3 3.7 %collective-permute-start.19 = (f32[160,128]{1,0:T(8,128)S(1)}, f32[160,128]{1,0:T(8,128)S(1)}, u32[]{:S(2)}, u32[]{:S(2)}) collective-permute-start(f32[160,128]{1,0:T(8,128)S(1)} %add_add_fusion.1), channel_id=1, source_target_pairs={{0,3},{1,2},{2,1},{3,0},{4,7},{5,6},{6,5},{7,4},{8,11},{9,10},{10,... | collective-permute-start | bytes 245768 | tf_op jit(solution)/shard_map/ppermute | solution.py:267
  51.6 1.6 %collective-permute-start.10 = (f32[416,128]{1,0:T(8,128)S(1)}, f32[416,128]{1,0:T(8,128)S(1)}, u32[]{:S(2)}, u32[]{:S(2)}) collective-permute-start(f32[416,128]{1,0:T(8,128)S(1)} %get-tuple-element.48), channel_id=1, source_target_pairs={{0,24},{4,28},{8,16},{12,20},{16,8},{20,12},{24,0},{28,4},{1,25},{... | collective-permute-start | bytes 638984 | tf_op jit(solution)/shard_map/ppermute | solution.py:267
  53.2 1.6 %collective-permute-done.18 = f32[160,128]{1,0:T(8,128)S(1)} collective-permute-done((f32[160,128]{1,0:T(8,128)S(1)}, f32[160,128]{1,0:T(8,128)S(1)}, u32[]{:S(2)}, u32[]{:S(2)}) %collective-permute-start.18) | collective-permute-done | bytes 81952 | tf_op jit(solution)/shard_map/ppermute | solution.py:267
  54.9 2.0 %collective-permute-done.8.refs_1_ = f32[416,128]{1,0:T(8,128)S(1)} collective-permute-done((f32[416,128]{1,0:T(8,128)S(1)}, f32[416,128]{1,0:T(8,128)S(1)}, u32[]{:S(2)}, u32[]{:S(2)}) %collective-permute-start.8) | collective-permute-done | bytes 213024 | tf_op jit(solution)/shard_map/ppermute | solution.py:267
  56.9 2.9 %collective-permute-done.9.refs_2_ = f32[416,128]{1,0:T(8,128)S(1)} collective-permute-done((f32[416,128]{1,0:T(8,128)S(1)}, f32[416,128]{1,0:T(8,128)S(1)}, u32[]{:S(2)}, u32[]{:S(2)}) %collective-permute-start.9) | collective-permute-done | bytes 213024 | tf_op jit(solution)/shard_map/ppermute | solution.py:267
  61.8 2.6 %collective-permute-start.12 = (f32[104,128]{1,0:T(8,128)S(1)}, f32[104,128]{1,0:T(8,128)S(1)}, u32[]{:S(2)}, u32[]{:S(2)}) collective-permute-start(f32[104,128]{1,0:T(8,128)S(1)} %get-tuple-element.51), channel_id=1, source_target_pairs={{0,2},{1,3},{2,0},{3,1},{4,6},{5,7},{6,4},{7,5},{8,10},{9,11},{10,... | collective-permute-start | bytes 159752 | tf_op jit(solution)/shard_map/ppermute | solution.py:267
  64.8 10.0 %all_gather.3.first_ref = f32[1280,128]{1,0:T(8,128)S(1)} all-gather(f32[160,128]{1,0:T(8,128)S(1)} %add_add_fusion), channel_id=1, replica_groups=mesh['band'=8,'ga'=4] {'band'}, dimensions={0}, use_global_device_ids=true | all-gather | bytes 737280 | tf_op jit(solution)/shard_map/all_gather | solution.py:293
  74.9 3.5 %collective-permute-start.22 = (f32[104,128]{1,0:T(8,128)S(1)}, f32[104,128]{1,0:T(8,128)S(1)}, u32[]{:S(2)}, u32[]{:S(2)}) collective-permute-start(f32[104,128]{1,0:T(8,128)S(1)} %add_add_fusion.2), channel_id=1, source_target_pairs={{0,3},{1,2},{2,1},{3,0},{4,7},{5,6},{6,5},{7,4},{8,11},{9,10},{10,... | collective-permute-start | bytes 159752 | tf_op jit(solution)/shard_map/ppermute | solution.py:267
  79.4 7.4 %shard_map.20 = (f32[256,256]{1,0:T(8,128)S(1)}, f32[256,512]{1,0:T(8,128)S(1)}, f32[8,128]{1,0:T(8,128)S(1)}) custom-call(s32[3]{0:T(128)S(1)} %pad_add_fusion.idx_ref, f32[1280,128]{1,0:T(8,128)S(1)} %all_gather.3.first_ref), custom_call_target="tpu_custom_call" | custom-call | flops 3000000000 | tf_op jit(solution)/shard_map/pallas_call | solution.py:126
  86.9 1.5 %collective-permute-start.25 = (f32[416,128]{1,0:T(8,128)S(1)}, f32[416,128]{1,0:T(8,128)S(1)}, u32[]{:S(2)}, u32[]{:S(2)}) collective-permute-start(f32[416,128]{1,0:T(8,128)S(1)} %pad_maximum_fusion), channel_id=1, source_target_pairs={{0,24},{4,28},{8,16},{12,20},{16,8},{20,12},{24,0},{28,4},{1,25},{... | collective-permute-start | bytes 638984 | tf_op jit(solution)/shard_map/ppermute | solution.py:267
  90.4 6.9 %shard_map.21 = (f32[256,512]{1,0:T(8,128)S(1)}, f32[8,128]{1,0:T(8,128)S(1)}) custom-call(s32[3]{0:T(128)S(1)} %pad_add_fusion.idx_ref, f32[256,512]{1,0:T(8,128)S(1)} %get-tuple-element.59.in_ref, f32[8,128]{1,0:T(8,128)S(1)} %get-tuple-element.62.before_ref), custom_call_target="tpu_custom_call" | custom-call | flops 3000000000 | tf_op jit(solution)/shard_map/pallas_call | solution.py:126
  97.3 1.7 %collective-permute-done.24 = f32[416,128]{1,0:T(8,128)S(1)} collective-permute-done((f32[416,128]{1,0:T(8,128)S(1)}, f32[416,128]{1,0:T(8,128)S(1)}, u32[]{:S(2)}, u32[]{:S(2)}) %collective-permute-start.24) | collective-permute-done | bytes 213024 | tf_op jit(solution)/shard_map/ppermute | solution.py:267
  99.2 2.4 %collective-permute-done.26.far_ref = f32[1664,128]{1,0:T(8,128)S(1)} collective-permute-done((f32[1664,128]{1,0:T(8,128)S(1)}, f32[1664,128]{1,0:T(8,128)S(1)}, u32[]{:S(2)}, u32[]{:S(2)}) %collective-permute-start.26) | collective-permute-done | bytes 852000 | tf_op jit(solution)/shard_map/ppermute | solution.py:267
  101.6 17.3 %shard_map.22 = (f32[128,512]{1,0:T(8,128)S(1)}, f32[128,512]{1,0:T(8,128)S(1)}, f32[128,512]{1,0:T(8,128)S(1)}, f32[128,512]{1,0:T(8,128)S(1)}, f32[128,512]{1,...) custom-call(s32[3]{0:T(128)S(1)} %pad_add_fusion.idx_ref, ...), custom_call_target="tpu_custom_call" | custom-call | flops 24999999488 | tf_op jit(solution)/shard_map/pallas_call | solution.py:126
  124.4 3.9 %collective-permute-done.32.refs_2_ = f32[128,512]{1,0:T(8,128)S(1)} collective-permute-done((f32[128,512]{1,0:T(8,128)S(1)}, f32[128,512]{1,0:T(8,128)S(1)}, u32[]{:S(2)}, u32[]{:S(2)}) %collective-permute-start.32) | collective-permute-done | bytes 262176 | tf_op jit(solution)/shard_map/ppermute | solution.py:267
  128.4 4.4 %collective-permute-done.33.refs_3_ = f32[128,512]{1,0:T(8,128)S(1)} collective-permute-done((f32[128,512]{1,0:T(8,128)S(1)}, f32[128,512]{1,0:T(8,128)S(1)}, u32[]{:S(2)}, u32[]{:S(2)}) %collective-permute-start.33) | collective-permute-done | bytes 262176 | tf_op jit(solution)/shard_map/ppermute | solution.py:267
  132.8 1.5 %shard_map.23.refs_4_ = f32[128,4096]{1,0:T(8,128)} custom-call(s32[3]{0:T(128)S(1)} %pad_add_fusion.idx_ref, f32[128,512]{1,0:T(8,128)S(1)} %get-tuple-element.77.refs_0_, f32[128,512]{1,0:T(8,128)S(1)} %collective-permute-done.31.refs_1_, f32[128,512]{1,0:T(8,128)S(1)} %collective-permute-done.32.refs_2_, f32[128,512]{1,0:T(8,128)S(1)} %collective-permute-done.33.refs_3_), custom_call_target="tpu_custom_call" | custom-call | tf_op jit(solution)/shard_map/pallas_call | solution.py:169
  134.3 9.5 %collective-permute-done.28.refs_1_ = f32[128,512]{1,0:T(8,128)S(1)} collective-permute-done((f32[128,512]{1,0:T(8,128)S(1)}, f32[128,512]{1,0:T(8,128)S(1)}, u32[]{:S(2)}, u32[]{:S(2)}) %collective-permute-start.28) | collective-permute-done | bytes 262176 | tf_op jit(solution)/shard_map/ppermute | solution.py:267
  144.5 1.5 %shard_map.24 = f32[128,4096]{1,0:T(8,128)} custom-call(s32[3]{0:T(128)S(1)} %pad_add_fusion.idx_ref, f32[128,512]{1,0:T(8,128)S(1)} %collective-permute-done.27.refs_0_, f32[128,512]{1,0:T(8,128)S(1)} %collective-permute-done.28.refs_1_, f32[128,512]{1,0:T(8,128)S(1)} %collective-permute-done.29.refs_2_, ...), custom_call_target="tpu_custom_call", output_to_operand_aliasing={{}: (5, {})} | custom-call | tf_op jit(solution)/shard_map/pallas_call | solution.py:169
  (55 shorter events, 20.9 us)
Async XLA Ops:
  1.8 10.1 %collective-permute-start.6 = (f32[128,512]{1,0:T(8,128)S(1)}, f32[128,512]{1,0:T(8,128)S(1)}, u32[]{:S(2)}, u32[]{:S(2)}) collective-permute-start(f32[128,512]{1,0:T(8,128)S(1)} %get-tuple-element.81), channel_id=1, source_target_pairs={{0,28},{4,24},{8,20},{12,16},{16,12},{20,8},{24,4},{28,0},{1,29},{... | collective-permute-start | bytes 786440 | tf_op jit(solution)/shard_map/ppermute | solution.py:267
  5.2 12.4 %collective-permute-start.4 = (f32[128,512]{1,0:T(8,128)S(1)}, f32[128,512]{1,0:T(8,128)S(1)}, u32[]{:S(2)}, u32[]{:S(2)}) collective-permute-start(f32[128,512]{1,0:T(8,128)S(1)} %get-tuple-element.82), channel_id=1, source_target_pairs={{0,20},{4,16},{8,28},{12,24},{16,4},{20,0},{24,12},{28,8},{1,21},{... | collective-permute-start | bytes 786440 | tf_op jit(solution)/shard_map/ppermute | solution.py:267
  6.0 18.1 %collective-permute-start.3 = (f32[128,512]{1,0:T(8,128)S(1)}, f32[128,512]{1,0:T(8,128)S(1)}, u32[]{:S(2)}, u32[]{:S(2)}) collective-permute-start(f32[128,512]{1,0:T(8,128)S(1)} %get-tuple-element.83), channel_id=1, source_target_pairs={{0,16},{4,20},{8,24},{12,28},{16,0},{20,4},{24,8},{28,12},{1,17},{... | collective-permute-start | bytes 786440 | tf_op jit(solution)/shard_map/ppermute | solution.py:267
  7.5 16.6 %collective-permute-start.2 = (f32[128,512]{1,0:T(8,128)S(1)}, f32[128,512]{1,0:T(8,128)S(1)}, u32[]{:S(2)}, u32[]{:S(2)}) collective-permute-start(f32[128,512]{1,0:T(8,128)S(1)} %get-tuple-element.84), channel_id=1, source_target_pairs={{0,12},{4,8},{8,4},{12,0},{16,28},{20,24},{24,20},{28,16},{1,13},{... | collective-permute-start | bytes 786440 | tf_op jit(solution)/shard_map/ppermute | solution.py:267
  7.5 16.7 %collective-permute-start.1 = (f32[128,512]{1,0:T(8,128)S(1)}, f32[128,512]{1,0:T(8,128)S(1)}, u32[]{:S(2)}, u32[]{:S(2)}) collective-permute-start(f32[128,512]{1,0:T(8,128)S(1)} %get-tuple-element.85), channel_id=1, source_target_pairs={{0,8},{4,12},{8,0},{12,4},{16,24},{20,28},{24,16},{28,20},{1,9},{5... | collective-permute-start | bytes 786440 | tf_op jit(solution)/shard_map/ppermute | solution.py:267
  11.9 12.2 %collective-permute-start = (f32[128,512]{1,0:T(8,128)S(1)}, f32[128,512]{1,0:T(8,128)S(1)}, u32[]{:S(2)}, u32[]{:S(2)}) collective-permute-start(f32[128,512]{1,0:T(8,128)S(1)} %get-tuple-element.86), channel_id=1, source_target_pairs={{0,4},{4,0},{8,12},{12,8},{16,20},{20,16},{24,28},{28,24},{1,5},{5... | collective-permute-start | bytes 786440 | tf_op jit(solution)/shard_map/ppermute | solution.py:267
  17.6 11.4 %collective-permute-start.5 = (f32[128,512]{1,0:T(8,128)S(1)}, f32[128,512]{1,0:T(8,128)S(1)}, u32[]{:S(2)}, u32[]{:S(2)}) collective-permute-start(f32[128,512]{1,0:T(8,128)S(1)} %get-tuple-element.88), channel_id=1, source_target_pairs={{0,24},{4,28},{8,16},{12,20},{16,8},{20,12},{24,0},{28,4},{1,25},{... | collective-permute-start | bytes 786440 | tf_op jit(solution)/shard_map/ppermute | solution.py:267
  36.1 5.1 %collective-permute-start.14 = (f32[160,128]{1,0:T(8,128)S(1)}, f32[160,128]{1,0:T(8,128)S(1)}, u32[]{:S(2)}, u32[]{:S(2)}) collective-permute-start(f32[160,128]{1,0:T(8,128)S(1)} %get-tuple-element.54), channel_id=1, source_target_pairs={{0,8},{4,12},{8,0},{12,4},{16,24},{20,28},{24,16},{28,20},{1,9},{5... | collective-permute-start | bytes 245768 | tf_op jit(solution)/shard_map/ppermute | solution.py:267
  38.4 5.3 %collective-permute-start.15 = (f32[160,128]{1,0:T(8,128)S(1)}, f32[160,128]{1,0:T(8,128)S(1)}, u32[]{:S(2)}, u32[]{:S(2)}) collective-permute-start(f32[160,128]{1,0:T(8,128)S(1)} %get-tuple-element.55), channel_id=1, source_target_pairs={{0,16},{4,20},{8,24},{12,28},{16,0},{20,4},{24,8},{28,12},{1,17},{... | collective-permute-start | bytes 245768 | tf_op jit(solution)/shard_map/ppermute | solution.py:267
  39.9 5.3 %collective-permute-start.16 = (f32[160,128]{1,0:T(8,128)S(1)}, f32[160,128]{1,0:T(8,128)S(1)}, u32[]{:S(2)}, u32[]{:S(2)}) collective-permute-start(f32[160,128]{1,0:T(8,128)S(1)} %get-tuple-element.56), channel_id=1, source_target_pairs={{0,24},{4,28},{8,16},{12,20},{16,8},{20,12},{24,0},{28,4},{1,25},{... | collective-permute-start | bytes 245768 | tf_op jit(solution)/shard_map/ppermute | solution.py:267
  45.3 6.3 %collective-permute-start.19 = (f32[160,128]{1,0:T(8,128)S(1)}, f32[160,128]{1,0:T(8,128)S(1)}, u32[]{:S(2)}, u32[]{:S(2)}) collective-permute-start(f32[160,128]{1,0:T(8,128)S(1)} %add_add_fusion.1), channel_id=1, source_target_pairs={{0,3},{1,2},{2,1},{3,0},{4,7},{5,6},{6,5},{7,4},{8,11},{9,10},{10,... | collective-permute-start | bytes 245768 | tf_op jit(solution)/shard_map/ppermute | solution.py:267
  48.9 5.9 %collective-permute-start.18 = (f32[160,128]{1,0:T(8,128)S(1)}, f32[160,128]{1,0:T(8,128)S(1)}, u32[]{:S(2)}, u32[]{:S(2)}) collective-permute-start(f32[160,128]{1,0:T(8,128)S(1)} %add_add_fusion.1), channel_id=1, source_target_pairs={{0,2},{1,3},{2,0},{3,1},{4,6},{5,7},{6,4},{7,5},{8,10},{9,11},{10,... | collective-permute-start | bytes 245768 | tf_op jit(solution)/shard_map/ppermute | solution.py:267
  48.9 5.9 %collective-permute-start.17 = (f32[160,128]{1,0:T(8,128)S(1)}, f32[160,128]{1,0:T(8,128)S(1)}, u32[]{:S(2)}, u32[]{:S(2)}) collective-permute-start(f32[160,128]{1,0:T(8,128)S(1)} %add_add_fusion.1), channel_id=1, source_target_pairs={{0,1},{1,0},{2,3},{3,2},{4,5},{5,4},{6,7},{7,6},{8,9},{9,8},{10,11... | collective-permute-start | bytes 245768 | tf_op jit(solution)/shard_map/ppermute | solution.py:267
  49.7 7.2 %collective-permute-start.8 = (f32[416,128]{1,0:T(8,128)S(1)}, f32[416,128]{1,0:T(8,128)S(1)}, u32[]{:S(2)}, u32[]{:S(2)}) collective-permute-start(f32[416,128]{1,0:T(8,128)S(1)} %get-tuple-element.46), channel_id=1, source_target_pairs={{0,8},{4,12},{8,0},{12,4},{16,24},{20,28},{24,16},{28,20},{1,9},{5... | collective-permute-start | bytes 638984 | tf_op jit(solution)/shard_map/ppermute | solution.py:267
  50.3 9.5 %collective-permute-start.9 = (f32[416,128]{1,0:T(8,128)S(1)}, f32[416,128]{1,0:T(8,128)S(1)}, u32[]{:S(2)}, u32[]{:S(2)}) collective-permute-start(f32[416,128]{1,0:T(8,128)S(1)} %get-tuple-element.47), channel_id=1, source_target_pairs={{0,16},{4,20},{8,24},{12,28},{16,0},{20,4},{24,8},{28,12},{1,17},{... | collective-permute-start | bytes 638984 | tf_op jit(solution)/shard_map/ppermute | solution.py:267
  51.6 8.2 %collective-permute-start.10 = (f32[416,128]{1,0:T(8,128)S(1)}, f32[416,128]{1,0:T(8,128)S(1)}, u32[]{:S(2)}, u32[]{:S(2)}) collective-permute-start(f32[416,128]{1,0:T(8,128)S(1)} %get-tuple-element.48), channel_id=1, source_target_pairs={{0,24},{4,28},{8,16},{12,20},{16,8},{20,12},{24,0},{28,4},{1,25},{... | collective-permute-start | bytes 638984 | tf_op jit(solution)/shard_map/ppermute | solution.py:267
  60.4 14.5 %collective-permute-start.11 = (f32[104,128]{1,0:T(8,128)S(1)}, f32[104,128]{1,0:T(8,128)S(1)}, u32[]{:S(2)}, u32[]{:S(2)}) collective-permute-start(f32[104,128]{1,0:T(8,128)S(1)} %get-tuple-element.50), channel_id=1, source_target_pairs={{0,1},{1,0},{2,3},{3,2},{4,5},{5,4},{6,7},{7,6},{8,9},{9,8},{10,11... | collective-permute-start | bytes 159752 | tf_op jit(solution)/shard_map/ppermute | solution.py:267
  61.8 13.1 %collective-permute-start.12 = (f32[104,128]{1,0:T(8,128)S(1)}, f32[104,128]{1,0:T(8,128)S(1)}, u32[]{:S(2)}, u32[]{:S(2)}) collective-permute-start(f32[104,128]{1,0:T(8,128)S(1)} %get-tuple-element.51), channel_id=1, source_target_pairs={{0,2},{1,3},{2,0},{3,1},{4,6},{5,7},{6,4},{7,5},{8,10},{9,11},{10,... | collective-permute-start | bytes 159752 | tf_op jit(solution)/shard_map/ppermute | solution.py:267
  64.4 10.4 %collective-permute-start.13 = (f32[104,128]{1,0:T(8,128)S(1)}, f32[104,128]{1,0:T(8,128)S(1)}, u32[]{:S(2)}, u32[]{:S(2)}) collective-permute-start(f32[104,128]{1,0:T(8,128)S(1)} %get-tuple-element.52), channel_id=1, source_target_pairs={{0,3},{1,2},{2,1},{3,0},{4,7},{5,6},{6,5},{7,4},{8,11},{9,10},{10,... | collective-permute-start | bytes 159752 | tf_op jit(solution)/shard_map/ppermute | solution.py:267
  74.9 11.9 %collective-permute-start.22 = (f32[104,128]{1,0:T(8,128)S(1)}, f32[104,128]{1,0:T(8,128)S(1)}, u32[]{:S(2)}, u32[]{:S(2)}) collective-permute-start(f32[104,128]{1,0:T(8,128)S(1)} %add_add_fusion.2), channel_id=1, source_target_pairs={{0,3},{1,2},{2,1},{3,0},{4,7},{5,6},{6,5},{7,4},{8,11},{9,10},{10,... | collective-permute-start | bytes 159752 | tf_op jit(solution)/shard_map/ppermute | solution.py:267
  78.4 8.5 %collective-permute-start.21 = (f32[104,128]{1,0:T(8,128)S(1)}, f32[104,128]{1,0:T(8,128)S(1)}, u32[]{:S(2)}, u32[]{:S(2)}) collective-permute-start(f32[104,128]{1,0:T(8,128)S(1)} %add_add_fusion.2), channel_id=1, source_target_pairs={{0,2},{1,3},{2,0},{3,1},{4,6},{5,7},{6,4},{7,5},{8,10},{9,11},{10,... | collective-permute-start | bytes 159752 | tf_op jit(solution)/shard_map/ppermute | solution.py:267
  78.4 8.5 %collective-permute-start.20 = (f32[104,128]{1,0:T(8,128)S(1)}, f32[104,128]{1,0:T(8,128)S(1)}, u32[]{:S(2)}, u32[]{:S(2)}) collective-permute-start(f32[104,128]{1,0:T(8,128)S(1)} %add_add_fusion.2), channel_id=1, source_target_pairs={{0,1},{1,0},{2,3},{3,2},{4,5},{5,4},{6,7},{7,6},{8,9},{9,8},{10,11... | collective-permute-start | bytes 159752 | tf_op jit(solution)/shard_map/ppermute | solution.py:267
  86.9 10.5 %collective-permute-start.25 = (f32[416,128]{1,0:T(8,128)S(1)}, f32[416,128]{1,0:T(8,128)S(1)}, u32[]{:S(2)}, u32[]{:S(2)}) collective-permute-start(f32[416,128]{1,0:T(8,128)S(1)} %pad_maximum_fusion), channel_id=1, source_target_pairs={{0,24},{4,28},{8,16},{12,20},{16,8},{20,12},{24,0},{28,4},{1,25},{... | collective-permute-start | bytes 638984 | tf_op jit(solution)/shard_map/ppermute | solution.py:267
  88.4 10.7 %collective-permute-start.24 = (f32[416,128]{1,0:T(8,128)S(1)}, f32[416,128]{1,0:T(8,128)S(1)}, u32[]{:S(2)}, u32[]{:S(2)}) collective-permute-start(f32[416,128]{1,0:T(8,128)S(1)} %pad_maximum_fusion), channel_id=1, source_target_pairs={{0,16},{4,20},{8,24},{12,28},{16,0},{20,4},{24,8},{28,12},{1,17},{... | collective-permute-start | bytes 638984 | tf_op jit(solution)/shard_map/ppermute | solution.py:267
  89.3 9.8 %collective-permute-start.23 = (f32[416,128]{1,0:T(8,128)S(1)}, f32[416,128]{1,0:T(8,128)S(1)}, u32[]{:S(2)}, u32[]{:S(2)}) collective-permute-start(f32[416,128]{1,0:T(8,128)S(1)} %pad_maximum_fusion), channel_id=1, source_target_pairs={{0,8},{4,12},{8,0},{12,4},{16,24},{20,28},{24,16},{28,20},{1,9},{5... | collective-permute-start | bytes 638984 | tf_op jit(solution)/shard_map/ppermute | solution.py:267
  118.9 4.0 %collective-permute-start.31 = (f32[128,512]{1,0:T(8,128)S(1)}, f32[128,512]{1,0:T(8,128)S(1)}, u32[]{:S(2)}, u32[]{:S(2)}) collective-permute-start(f32[128,512]{1,0:T(8,128)S(1)} %get-tuple-element.78), channel_id=1, source_target_pairs={{0,4},{4,0},{8,12},{12,8},{16,20},{20,16},{24,28},{28,24},{1,5},{5... | collective-permute-start | bytes 786440 | tf_op jit(solution)/shard_map/ppermute | solution.py:267
  119.2 9.1 %collective-permute-start.32 = (f32[128,512]{1,0:T(8,128)S(1)}, f32[128,512]{1,0:T(8,128)S(1)}, u32[]{:S(2)}, u32[]{:S(2)}) collective-permute-start(f32[128,512]{1,0:T(8,128)S(1)} %get-tuple-element.79), channel_id=1, source_target_pairs={{0,8},{4,12},{8,0},{12,4},{16,24},{20,28},{24,16},{28,20},{1,9},{5... | collective-permute-start | bytes 786440 | tf_op jit(solution)/shard_map/ppermute | solution.py:267
  120.1 14.3 %collective-permute-start.27 = (f32[128,512]{1,0:T(8,128)S(1)}, f32[128,512]{1,0:T(8,128)S(1)}, u32[]{:S(2)}, u32[]{:S(2)}) collective-permute-start(f32[128,512]{1,0:T(8,128)S(1)} %get-tuple-element.73), channel_id=1, source_target_pairs={{0,16},{4,20},{8,24},{12,28},{16,0},{20,4},{24,8},{28,12},{1,17},{... | collective-permute-start | bytes 786440 | tf_op jit(solution)/shard_map/ppermute | solution.py:267
  121.2 22.7 %collective-permute-start.28 = (f32[128,512]{1,0:T(8,128)S(1)}, f32[128,512]{1,0:T(8,128)S(1)}, u32[]{:S(2)}, u32[]{:S(2)}) collective-permute-start(f32[128,512]{1,0:T(8,128)S(1)} %get-tuple-element.74), channel_id=1, source_target_pairs={{0,20},{4,16},{8,28},{12,24},{16,4},{20,0},{24,12},{28,8},{1,21},{... | collective-permute-start | bytes 786440 | tf_op jit(solution)/shard_map/ppermute | solution.py:267
  121.5 11.3 %collective-permute-start.33 = (f32[128,512]{1,0:T(8,128)S(1)}, f32[128,512]{1,0:T(8,128)S(1)}, u32[]{:S(2)}, u32[]{:S(2)}) collective-permute-start(f32[128,512]{1,0:T(8,128)S(1)} %get-tuple-element.80), channel_id=1, source_target_pairs={{0,12},{4,8},{8,4},{12,0},{16,28},{20,24},{24,20},{28,16},{1,13},{... | collective-permute-start | bytes 786440 | tf_op jit(solution)/shard_map/ppermute | solution.py:267
  122.9 20.9 %collective-permute-start.29 = (f32[128,512]{1,0:T(8,128)S(1)}, f32[128,512]{1,0:T(8,128)S(1)}, u32[]{:S(2)}, u32[]{:S(2)}) collective-permute-start(f32[128,512]{1,0:T(8,128)S(1)} %get-tuple-element.75), channel_id=1, source_target_pairs={{0,24},{4,28},{8,16},{12,20},{16,8},{20,12},{24,0},{28,4},{1,25},{... | collective-permute-start | bytes 786440 | tf_op jit(solution)/shard_map/ppermute | solution.py:267
  128.3 16.2 %collective-permute-start.30 = (f32[128,512]{1,0:T(8,128)S(1)}, f32[128,512]{1,0:T(8,128)S(1)}, u32[]{:S(2)}, u32[]{:S(2)}) collective-permute-start(f32[128,512]{1,0:T(8,128)S(1)} %get-tuple-element.76), channel_id=1, source_target_pairs={{0,28},{4,24},{8,20},{12,16},{16,12},{20,8},{24,4},{28,0},{1,29},{... | collective-permute-start | bytes 786440 | tf_op jit(solution)/shard_map/ppermute | solution.py:267
  (2 other events, 5.4 us)
